TPU v7x, 32 devices: a whole 2x2x4 slice. The times are simulated.
32 devices in a mesh: visit: 4 (over y, x), raft: 8 (over z, core).
Axes of the slice: x: 2, y: 2, z: 4, core: 2. Of those that a mesh axis runs over, the one named last changes fastest.
Arguments:
- tiles: bfloat16 [3072, 16384], P(('visit', 'raft')), may hold values from -6 to 6
- weights: float32 [3072], P(('visit', 'raft')), may hold values from 0.25 to 4
- coef: float32 [3072, 27], P(('visit', 'raft')), may hold values from -4 to 4
- owner: int32 [3072, 1], P(('visit', 'raft')), may hold values from 0 to 7; in each aligned block of 96 rows (0 to 95, 96 to 191, ...) at most 24 rows name the same one
- patch: int32 [3072], P(('visit', 'raft')), may hold values from 0 to 23
- row_taps: bfloat16 [27, 41], replicated, may hold values from -1 to 1
- col_taps: bfloat16 [27, 41], replicated, may hold values from -1 to 1
Outputs:
- coadd_image: float32 [8, 24, 128, 128], P('raft', 'visit')
Inputs may be any that keep to these rules, and one draw needn't show every extreme that they name: Among the 96 tiles of one device (aligned blocks of rows in order), at most 24 name the same owner; in some blocks one owner is named by exactly 24.
All inputs are finite; a program needn't handle non-finite values.
Results may differ from a plain program's by a relative error of at most 0.0052.
Values may be sent and summed in bfloat16 or wider, within the bound.
A program may use at most 192 MiB of HBM per device.

v0:
```python
import jax
import jax.numpy as jnp
from jax import lax
from jax.sharding import PartitionSpec as P

SIDE = 128
KERNEL = 41
NB = 27
PATCH_DEV = 24


def with_halo(shard, sides, width):
    for axis, dim in sides:
        size, length = (lax.axis_size(axis), shard.shape[dim])
        up = [(i, (i + 1) % size) for i in range(size - 1)]
        down = [(j, i) for i, j in up]
        last = lax.slice_in_dim(shard, length - width, length, axis=dim)
        leading = lax.slice_in_dim(shard, 0, width, axis=dim)
        before = lax.ppermute(last, axis, up)
        after = lax.ppermute(leading, axis, down)
        shard = jnp.concatenate([before, shard, after], axis=dim)
    return shard


def tap_band(tap_values, offsets):
    selector = (offsets[:, :, None] == jnp.arange(tap_values.shape[1])[None, None, :]).astype(
        jnp.float32
    )
    return jnp.einsum("qrj,bj->bqr", selector, tap_values.astype(jnp.float32)).astype(jnp.bfloat16)


def body(tiles, weights, coef, owner, patch, row_taps, col_taps):
    tile_count = tiles.shape[0]
    peer_count = lax.axis_size("raft")
    capacity = max(2, 2 * tile_count // peer_count)
    half_width = (KERNEL - 1) // 2
    owner_ids = owner[:, 0]
    owner_hits = (owner_ids[:, None] == jnp.arange(peer_count)[None, :]).astype(jnp.int32)
    slot_rank = jnp.sum(jnp.cumsum(owner_hits, axis=0) * owner_hits, axis=1) - 1
    slot_index = owner_ids * capacity + slot_rank
    placing = (jnp.arange(peer_count * capacity)[:, None] == slot_index[None, :]).astype(
        jnp.bfloat16
    )
    scaled = (weights[:, None] * coef).astype(jnp.bfloat16)
    plain_weight = weights.astype(jnp.bfloat16)[:, None]
    tile_terms = jnp.concatenate([scaled, plain_weight], axis=1)
    patch_hits = (patch[:, None] == jnp.arange(PATCH_DEV)[None, :]).astype(jnp.bfloat16)
    mixing = (tile_terms[:, :, None] * patch_hits[:, None, :]).reshape(
        tile_count, (NB + 1) * PATCH_DEV
    )
    send_tiles = jnp.dot(placing, tiles, preferred_element_type=jnp.float32).astype(jnp.bfloat16)
    send_mixing = jnp.dot(placing, mixing, preferred_element_type=jnp.float32).astype(jnp.bfloat16)
    got_tiles, got_mixing = (
        lax.all_to_all(send_tiles, "raft", split_axis=0, concat_axis=0, tiled=True),
        lax.all_to_all(send_mixing, "raft", split_axis=0, concat_axis=0, tiled=True),
    )
    planes = lax.dot_general(
        got_mixing[:, : NB * PATCH_DEV],
        got_tiles,
        (((0,), (0,)), ((), ())),
        preferred_element_type=jnp.float32,
    )
    planes = planes.astype(jnp.bfloat16).reshape(NB, PATCH_DEV, SIDE, SIDE)
    weight_sum = jnp.sum(got_mixing[:, NB * PATCH_DEV :].astype(jnp.float32), axis=0)
    blank_rim = jnp.zeros((NB, 1, SIDE, half_width), jnp.bfloat16)
    left_rim = jnp.concatenate([blank_rim, planes[:, :-1, :, SIDE - half_width :]], axis=1)
    right_rim = jnp.concatenate([planes[:, 1:, :, :half_width], blank_rim], axis=1)
    window = jnp.concatenate([left_rim, planes, right_rim], axis=3)
    wide_index = jnp.arange(SIDE + 2 * half_width)
    narrow = jnp.arange(SIDE)
    col_band = tap_band(col_taps, wide_index[:, None] - narrow[None, :])
    filtered = jnp.einsum(
        "bpyc,bcx->bpyx", window, col_band, preferred_element_type=jnp.float32
    ).astype(jnp.bfloat16)
    padded = with_halo(filtered, (("raft", 2),), half_width)
    row_band = tap_band(row_taps, wide_index[None, :] - narrow[:, None])
    stacked = jnp.einsum("byr,bprx->pyx", row_band, padded, preferred_element_type=jnp.float32)
    summed, weight_total = (
        lax.psum_scatter(stacked, "visit", scatter_dimension=0, tiled=True),
        lax.psum_scatter(weight_sum, "visit", scatter_dimension=0, tiled=True),
    )
    coadd_image = summed / (1.0 + weight_total)[:, None, None]
    return coadd_image[None]


def solution(mesh):
    placed = (
        P(("visit", "raft"), None),
        P(("visit", "raft")),
        P(("visit", "raft"), None),
        P(("visit", "raft"), None),
        P(("visit", "raft")),
        P(),
        P(),
    )
    return jax.shard_map(
        body, mesh=mesh, in_specs=placed, out_specs=P("raft", "visit", None, None), check_vma=False
    )
```

profile of v0, /device:TPU:3, one launch (start us, length us, event | category | flops | bytes accessed | tf_op | source)
XLA Modules:
  0.0 365.3 jit_solution(10164254434453762152)
XLA Ops:
  6.5 0.0 copy-start
  6.5 0.9 fusion.39
  7.4 0.1 reduce_window_sum.11
  7.6 0.8 select_reduce_fusion
  8.4 0.7 add_add_fusion
  9.1 0.7 convert_bitcast_fusion.1
  9.7 0.7 multiply_convert_fusion
  10.5 0.7 fusion.40
  11.2 1.0 convolution_convert_fusion.2
  12.1 5.5 %all-to-all-start = ((bf16[8,24,672]{2,1,0:T(8,128)(2,1)}), bf16[8,24,672]{2,1,0:T(8,128)(2,1)S(1)}, u32[]{:S(2)}, u32[]{:S(2)}) async-start(bf16[8,24,672]{2,1,0:T(8,128)(2,1)} %bitcast.41), calls=%async_computation | async-start | bytes 589824 | tf_op jit(solution)/shard_map/all_to_all | solution.py:55
  17.7 0.0 copy-done
  17.7 4.4 %convolution_convert_fusion.1 = bf16[192,16384]{1,0:T(8,128)(2,1)} fusion(bf16[96,16384]{1,0:T(8,128)(2,1)S(1)} %copy-done, s32[96]{0:T(128)S(1)} %add_add_fusion), kind=kOutput, calls=%fused_computation.19 | convolution fusion | flops 607143936 | bytes 9437568 | tf_op jit(solution)/shard_map/dot_general | solution.py:51
  22.1 4.9 %all-to-all-done = bf16[8,24,672]{2,1,0:T(8,128)(2,1)S(1)} async-done(((bf16[8,24,672]{2,1,0:T(8,128)(2,1)}), bf16[8,24,672]{2,1,0:T(8,128)(2,1)S(1)}, u32[]{:S(2)}, u32[]{:S(2)}) %all-to-all-start) | async-done | bytes 258080 | tf_op jit(solution)/shard_map/all_to_all | solution.py:55
  27.0 0.0 copy-start.2
  27.0 5.8 %all-to-all-start.1 = ((bf16[8,24,16384]{2,1,0:T(8,128)(2,1)}), bf16[8,24,16384]{2,1,0:T(8,128)(2,1)}, u32[]{:S(2)}, u32[]{:S(2)}) async-start(bf16[8,24,16384]{2,1,0:T(8,128)(2,1)} %bitcast.38), calls=%async_computation.1 | async-start | bytes 12582912 | tf_op jit(solution)/shard_map/all_to_all | solution.py:54
  32.9 0.0 reduce-scatter.2.cloned.1.call-start
  32.9 0.0 copy-done.2
  32.9 1.0 fusion.34
  33.9 137.2 %all-to-all-done.1 = bf16[8,24,16384]{2,1,0:T(8,128)(2,1)} async-done(((bf16[8,24,16384]{2,1,0:T(8,128)(2,1)}), bf16[8,24,16384]{2,1,0:T(8,128)(2,1)}, u32[]{:S(2)}, u32[]{:S(2)}) %all-to-all-start.1) | async-done | bytes 6291488 | tf_op jit(solution)/shard_map/all_to_all | solution.py:54
  171.1 12.0 %fusion.22 = bf16[81,8,128,128]{3,1,2,0:T(8,128)(2,1)} fusion(bf16[192,16384]{1,0:T(8,128)(2,1)} %bitcast.6, bf16[192,672]{1,0:T(8,128)(2,1)S(1)} %bitcast.39), kind=kOutput, calls=%fused_computation.22 | convolution fusion | flops 4087480320 | bytes 27783168 | tf_op jit(solution)/shard_map/dot_general | solution.py:57
  183.1 15.7 %copy.35 = bf16[81,8,128,128]{3,2,1,0:T(8,128)(2,1)} copy(bf16[81,8,128,128]{3,1,2,0:T(8,128)(2,1)} %fusion.22) | data formatting | bytes 42467328
  198.7 28.3 %copy.19 = bf16[27,24,128,128]{2,3,1,0:T(8,128)(2,1)} copy(bf16[27,24,128,128]{3,2,1,0:T(8,128)(2,1)} %bitcast.37) | data formatting | bytes 42467328 | tf_op jit(solution)/shard_map/reshape | solution.py:63
  227.0 5.4 %fusion.49 = (bf16[27,23,128,20]{2,3,1,0:T(8,128)(2,1)S(1)}, bf16[27,23,128,20]{2,3,1,0:T(8,128)(2,1)S(1)}) fusion(bf16[27,24,128,128]{2,3,1,0:T(8,128)(2,1)} %copy.19), kind=kLoop, calls=%fused_computation.63 | loop fusion | bytes 12718080 | tf_op jit(solution)/shard_map/slice | solution.py:66
  232.4 22.1 %fusion.19 = bf16[27,24,128,128]{3,2,1,0:T(8,128)(2,1)} fusion(bf16[27,23,128,20]{2,3,1,0:T(8,128)(2,1)S(1)} %get-tuple-element.8, bf16[27,23,128,20]{2,3,1,0:T(8,128)(2,1)S(1)} %get-tuple-element.7, bf16[27,24,128,128]{2,3,1,0:T(8,128)(2,1)} %copy.19, bf16[27,168,128,1]{2,0,1,3:T(8,128)(2,1)S(1)} %fusion.34), kind=kOutput, calls=%fused_computation.21 | convolution fusion | flops 3717218304 | bytes 49987584 | tf_op jit(solution)/shard_map/bpyc,bcx->bpyx/dot_general | solution.py:72
  254.6 4.7 %fusion.48 = (bf16[27,24,20,128]{3,2,1,0:T(8,128)(2,1)S(1)}, bf16[27,24,20,128]{3,2,1,0:T(8,128)(2,1)S(1)}) fusion(bf16[27,24,128,128]{3,2,1,0:T(8,128)(2,1)} %fusion.19), kind=kLoop, calls=%fused_computation.62 | loop fusion | bytes 13271040 | tf_op jit(solution)/shard_map/slice | solution.py:17
  259.3 0.0 copy-start.3
  259.3 0.4 copy.23
  259.7 2.1 collective-permute-start
  261.9 0.4 copy.24
  262.3 2.6 collective-permute-start.1
  264.9 0.0 copy-done.3
  264.9 2.7 convert_bitcast_fusion
  267.7 30.0 %collective-permute-done = bf16[27,24,20,128]{3,1,2,0:T(8,128)(2,1)S(1)} collective-permute-done((bf16[27,24,20,128]{3,1,2,0:T(8,128)(2,1)S(1)}, bf16[27,24,20,128]{3,1,2,0:T(8,128)(2,1)S(1)}, u32[]{:S(2)}, u32[]{:S(2)}) %collective-permute-start) | collective-permute-done | bytes 3317792 | tf_op jit(solution)/shard_map/ppermute | solution.py:19
  297.7 2.7 copy.25
  300.4 2.6 collective-permute-done.1
  303.0 2.7 copy.26
  305.8 0.0 copy-start.4
  305.8 0.0 copy-start.1
  305.8 20.4 %fusion.29 = f32[24,128,128]{1,2,0:T(8,128)} fusion(bf16[27,128,168,1]{2,0,1,3:T(8,128)(2,1)} %convert_bitcast_fusion, bf16[27,24,20,128]{3,2,1,0:T(8,128)(2,1)} %copy.26, bf16[27,24,128,128]{3,2,1,0:T(8,128)(2,1)} %fusion.19, bf16[27,24,20,128]{3,2,1,0:T(8,128)(2,1)} %copy.25), kind=kOutput, calls=%fused_computation.32 | convolution fusion | flops 3650863104 | bytes 30603264 | tf_op jit(solution)/shard_map/byr,bprx->pyx/dot_general | solution.py:77
  326.2 0.0 reduce-scatter.2.cloned.1.call-update
  326.2 0.0 copy-done.4
  326.2 0.6 dynamic-slice
  326.8 0.1 convert_reduce_fusion
  327.6 6.2 %all-reduce.2 = f32[24]{0:T(128)S(1)} all-reduce(f32[24]{0:T(128)S(1)} %convert_reduce_fusion), channel_id=3, replica_groups=mesh['visit'=4,'raft'=8] {'visit'}, use_global_device_ids=true, to_apply=%region_4.5.clone | all-reduce | flops 24 | bytes 192
  333.8 0.1 dynamic-slice_add_fusion
  333.8 22.6 %reduce-scatter.2.cloned.1.call-done = f32[6,128,128]{1,2,0:T(8,128)} async-done(((f32[24,128,128]{1,2,0:T(8,128)}), f32[6,128,128]{1,2,0:T(8,128)}) %reduce-scatter.2.cloned.1.call-update) | async-done | bytes 393232 | tf_op jit(solution)/shard_map/reduce_scatter | solution.py:79
  356.4 1.1 divide_bitcast_fusion
  357.5 0.9 copy.28
  358.4 0.0 copy-done.1
  (4 shorter events, 0.1 us)
Async XLA Ops:
  6.5 11.1 %copy-start = (bf16[96,16384]{1,0:T(8,128)(2,1)S(1)}, bf16[96,16384]{1,0:T(8,128)(2,1)}, u32[]{:S(2)}) copy-start(bf16[96,16384]{1,0:T(8,128)(2,1)} %param.7) | copy-start | bytes 9437188
  12.1 14.9 %all-to-all-start = ((bf16[8,24,672]{2,1,0:T(8,128)(2,1)}), bf16[8,24,672]{2,1,0:T(8,128)(2,1)S(1)}, u32[]{:S(2)}, u32[]{:S(2)}) async-start(bf16[8,24,672]{2,1,0:T(8,128)(2,1)} %bitcast.41), calls=%async_computation | async-start | bytes 589824 | tf_op jit(solution)/shard_map/all_to_all | solution.py:55
  27.0 5.9 %copy-start.2 = (bf16[27,41]{1,0:T(8,128)(2,1)S(1)}, bf16[27,41]{1,0:T(8,128)(2,1)}, u32[]{:S(2)}) copy-start(bf16[27,41]{1,0:T(8,128)(2,1)} %param.13) | copy-start | bytes 6646
  27.0 144.0 %all-to-all-start.1 = ((bf16[8,24,16384]{2,1,0:T(8,128)(2,1)}), bf16[8,24,16384]{2,1,0:T(8,128)(2,1)}, u32[]{:S(2)}, u32[]{:S(2)}) async-start(bf16[8,24,16384]{2,1,0:T(8,128)(2,1)} %bitcast.38), calls=%async_computation.1 | async-start | bytes 12582912 | tf_op jit(solution)/shard_map/all_to_all | solution.py:54
  32.9 323.5 %reduce-scatter.2.cloned.1.call-start = ((), (), s32[]{:S(2)}) async-start(), calls=%async_computation.3 | async-start | bytes 1966080 | tf_op jit(solution)/shard_map/reduce_scatter | solution.py:79
  259.3 5.7 %copy-start.3 = (bf16[27,41]{1,0:T(8,128)(2,1)S(1)}, bf16[27,41]{1,0:T(8,128)(2,1)}, u32[]{:S(2)}) copy-start(bf16[27,41]{1,0:T(8,128)(2,1)} %param.12) | copy-start | bytes 6646
  259.7 38.0 %collective-permute-start = (bf16[27,24,20,128]{3,1,2,0:T(8,128)(2,1)S(1)}, bf16[27,24,20,128]{3,1,2,0:T(8,128)(2,1)S(1)}, u32[]{:S(2)}, u32[]{:S(2)}) collective-permute-start(bf16[27,24,20,128]{3,1,2,0:T(8,128)(2,1)S(1)} %copy.23), channel_id=1, source_target_pairs={{0,1},{1,2},{2,3},{3,4},{4,5},{5,6},{6,7},{8,9},{9,10},{10,11},{11... | collective-permute-start | bytes 9953288 | tf_op jit(solution)/shard_map/ppermute | solution.py:19
  262.3 40.7 %collective-permute-start.1 = (bf16[27,24,20,128]{3,1,2,0:T(8,128)(2,1)S(1)}, bf16[27,24,20,128]{3,1,2,0:T(8,128)(2,1)S(1)}, u32[]{:S(2)}, u32[]{:S(2)}) collective-permute-start(bf16[27,24,20,128]{3,1,2,0:T(8,128)(2,1)S(1)} %copy.24), channel_id=1, source_target_pairs={{1,0},{2,1},{3,2},{4,3},{5,4},{6,5},{7,6},{9,8},{10,9},{11,10},{12... | collective-permute-start | bytes 9953288 | tf_op jit(solution)/shard_map/ppermute | solution.py:20
  305.8 20.5 %copy-start.4 = (u32[32]{0:T(128)S(1)}, u32[32]{0:T(128)}, u32[]{:S(2)}) copy-start(u32[32]{0:T(128)} %constant.23) | copy-start | bytes 388
  305.8 52.7 %copy-start.1 = (bf16[96,16384]{1,0:T(8,128)(2,1)S(1)}, bf16[96,16384]{1,0:T(8,128)(2,1)}, u32[]{:S(2)}) copy-start(bf16[96,16384]{1,0:T(8,128)(2,1)} %param.7) | copy-start | bytes 9437188
Sparse Core Ops, SparseCore 0:
  326.4 30.0 reduce-scatter.1
where the time goes:
time: 368 us; the launch traced here: 365 us
  waiting for transfers between devices  197 us (54%)
  matrix products  63.7 us (17%)
  local copies, waits for them, and re-layouts  61.9 us (17%)
  starting transfers between devices  16.1 us (4%)
  between operations  14.2 us (4%)
  blocking collectives  6.16 us (2%)
  other arithmetic  5.89 us (2%)
    all_to_all x1, waiting for transfers between devices, body(): lax.all_to_all(send_tiles, 'raft', split_axis=0, concat_axis=0, tiled=True)  137 us
    ppermute x1, waiting for transfers between devices, with_halo(): before = lax.ppermute(last, axis, up)  30 us
    reshape x1, local copies, waits for them, and re-layouts, body(): planes = planes.astype(jnp.bfloat16).reshape(NB, PATCH_DEV, SIDE, SIDE)  28.3 us
    reduce_scatter x1, waiting for transfers between devices, body(): lax.psum_scatter(stacked, 'visit', scatter_dimension=0, tiled=True)  22.6 us
    dot_general x1, matrix products, body(): jnp.einsum('bpyc,bcx->bpyx', window, col_band, preferred_element_type=jnp...  22.1 us
    dot_general x1, matrix products, body(): jnp.einsum('byr,bprx->pyx', row_band, padded, preferred_element_type=jnp....  20.4 us
    unnamed x12, local copies, waits for them, and re-layouts  16.3 us
    dot_general x1, matrix products, body(): lax.dot_general(got_mixing[:, :NB * PATCH_DEV], got_tiles, (((0,), (0,)),...  12 us
  transfers between devices with their start and end apart: 5, of which 5 were waited for; matrix products, arithmetic and copies ran while one was open for 3% of the time, Pallas kernels for 0%

commit v1 on v0

--- a/solution.py
+++ b/solution.py
@@ -1,12 +1,20 @@
+import functools
+
 import jax
 import jax.numpy as jnp
 from jax import lax
-from jax.sharding import PartitionSpec as P
+from jax.experimental import pallas as pl
+from jax.experimental.pallas import tpu as pltpu
+from jax.sharding import Mesh, PartitionSpec as P
 
 SIDE = 128
 KERNEL = 41
 NB = 27
 PATCH_DEV = 24
+GROUP = 9
+HALF = (KERNEL - 1) // 2
+TOP = 24
+OUT_ROWS = 176
 
 
 def with_halo(shard, sides, width):
@@ -83,7 +91,167 @@
     return coadd_image[None]
 
 
+def filter_kernel(mix_ref, got_ref, col_ref, row_ref, out_ref, planes, strip, filtered, total):
+    step = pl.program_id(0)
+    count = GROUP * PATCH_DEV
+    lines = got_ref.shape[1] // SIDE
+    blocks = PATCH_DEV + 1
+
+    def make_planes(pair, carry):
+        start = pl.multiple_of(pair * 2 * SIDE, 2 * SIDE)
+        both = jnp.dot(
+            mix_ref[...], got_ref[:, pl.ds(start, 2 * SIDE)], preferred_element_type=jnp.float32
+        )
+        row = pl.multiple_of(pair * 2 * count, 8)
+        planes[pl.ds(row, count), :] = both[:, :SIDE]
+        planes[pl.ds(pl.multiple_of(row + count, 8), count), :] = both[:, SIDE:]
+        return carry
+
+    lax.fori_loop(0, lines // 2, make_planes, 0, unroll=4)
+
+    @pl.when(step == 0)
+    def _():
+        strip[:, :SIDE] = jnp.zeros((lines, SIDE), jnp.bfloat16)
+        strip[:, (PATCH_DEV + 1) * SIDE :] = jnp.zeros((lines, SIDE), jnp.bfloat16)
+
+    def filter_columns(basis, carry):
+        for place in range(PATCH_DEV):
+            image = planes[pl.ds(basis * PATCH_DEV + place, lines, stride=count), :]
+            strip[:, (place + 1) * SIDE : (place + 2) * SIDE] = image.astype(jnp.bfloat16)
+        rows = pl.ds(pl.multiple_of(basis * lines, 16), lines)
+        for block in range(blocks):
+            wide = strip[:, block * SIDE : (block + 2) * SIDE]
+            filtered[rows, block * SIDE : (block + 1) * SIDE] = jnp.dot(
+                wide, col_ref[basis], preferred_element_type=jnp.float32
+            ).astype(jnp.bfloat16)
+        return carry
+
+    lax.fori_loop(0, GROUP, filter_columns, 0)
+
+    width = 5 * SIDE
+    for chunk in range(blocks // 5):
+        span = slice(chunk * width, (chunk + 1) * width)
+        part = jnp.dot(row_ref[0], filtered[:, span], preferred_element_type=jnp.float32)
+        total[:, span] = jnp.where(step == 0, part, total[:, span] + part)
+
+    @pl.when(step == NB // GROUP - 1)
+    def _():
+        for place in range(PATCH_DEV):
+            low = place * SIDE + SIDE // 2
+            out_ref[place] = total[:, low : low + SIDE].astype(jnp.bfloat16)
+
+
+def filter_tiles(mix, got, col_band, row_band):
+    slots, pixels = got.shape
+    lines = pixels // SIDE
+    steps = NB // GROUP
+    count = GROUP * PATCH_DEV
+    width = (PATCH_DEV + 1) * SIDE
+    return pl.pallas_call(
+        filter_kernel,
+        grid=(steps,),
+        out_shape=jax.ShapeDtypeStruct((PATCH_DEV, OUT_ROWS, SIDE), jnp.bfloat16),
+        in_specs=[
+            pl.BlockSpec((count, slots), lambda s: (s, 0)),
+            pl.BlockSpec((slots, pixels), lambda s: (0, 0)),
+            pl.BlockSpec((GROUP, 2 * SIDE, SIDE), lambda s: (s, 0, 0)),
+            pl.BlockSpec((1, OUT_ROWS, GROUP * lines), lambda s: (s, 0, 0)),
+        ],
+        out_specs=pl.BlockSpec((PATCH_DEV, OUT_ROWS, SIDE), lambda s: (0, 0, 0)),
+        scratch_shapes=[
+            pltpu.VMEM((lines * count, SIDE), jnp.float32),
+            pltpu.VMEM((lines, (PATCH_DEV + 2) * SIDE), jnp.bfloat16),
+            pltpu.VMEM((GROUP * lines, width), jnp.bfloat16),
+            pltpu.VMEM((OUT_ROWS, width), jnp.float32),
+        ],
+        compiler_params=pltpu.CompilerParams(vmem_limit_bytes=56 * 1024 * 1024),
+        cost_estimate=pl.CostEstimate(
+            flops=30_000_000_000, bytes_accessed=10_000_000, transcendentals=0
+        ),
+    )(mix, got, col_band, row_band)
+
+
+def plane_body(visits, depth, cores, tiles, weights, coef, owner, patch, row_taps, col_taps):
+    tile_count = tiles.shape[0]
+    owners = depth * cores
+    capacity = 2 * tile_count // owners
+    every = ("visit", "z", "core")
+    owner_ids = owner[:, 0]
+    plain_weight = weights.astype(jnp.bfloat16).astype(jnp.float32)
+    keys = owner_ids * PATCH_DEV + patch
+    key_hits = keys[:, None] == jnp.arange(owners * PATCH_DEV)[None, :]
+    weight_sum = jnp.sum(jnp.where(key_hits, plain_weight[:, None], 0.0), axis=0)
+    weight_total = lax.psum(weight_sum, every)
+    strip_id = lax.axis_index("z") * cores + lax.axis_index("core")
+    share = PATCH_DEV // visits
+    own_weight = lax.dynamic_slice(
+        weight_total, (strip_id * PATCH_DEV + lax.axis_index("visit") * share,), (share,)
+    )
+
+    owner_hits = (owner_ids[:, None] == jnp.arange(owners)[None, :]).astype(jnp.int32)
+    slot_rank = jnp.sum(jnp.cumsum(owner_hits, axis=0) * owner_hits, axis=1) - 1
+    slot_index = owner_ids * capacity + slot_rank
+    placing = (jnp.arange(owners * capacity)[:, None] == slot_index[None, :]).astype(jnp.bfloat16)
+    scaled = (weights[:, None] * coef).astype(jnp.bfloat16)
+    patch_hits = (patch[:, None] == jnp.arange(PATCH_DEV)[None, :]).astype(jnp.bfloat16)
+    blank = jnp.zeros((tile_count, SIDE - NB - PATCH_DEV), jnp.bfloat16)
+    terms = jnp.concatenate([scaled, patch_hits, blank], axis=1)
+    send_terms = jnp.dot(placing, terms, preferred_element_type=jnp.float32).astype(jnp.bfloat16)
+    send_tiles = jnp.dot(placing, tiles, preferred_element_type=jnp.float32).astype(jnp.bfloat16)
+    plane = ("visit", "core")
+    got_terms = lax.all_to_all(send_terms, plane, split_axis=0, concat_axis=0, tiled=True)
+    got_tiles = lax.all_to_all(send_tiles, plane, split_axis=0, concat_axis=0, tiled=True)
+    by_basis = got_terms[:, :NB].T
+    by_patch = got_terms[:, NB : NB + PATCH_DEV].T
+    mix = (by_basis[:, None, :] * by_patch[None, :, :]).reshape(NB * PATCH_DEV, -1)
+
+    wide_index = jnp.arange(2 * SIDE)
+    narrow = jnp.arange(SIDE)
+    col_band = tap_band(col_taps, wide_index[:, None] - narrow[None, :] - SIDE // 2 + HALF)
+    out_index = jnp.arange(OUT_ROWS)
+    row_band = tap_band(row_taps, narrow[None, :] - out_index[:, None] + TOP + HALF)
+    row_band = row_band.reshape(NB // GROUP, GROUP, OUT_ROWS, SIDE).transpose(0, 2, 1, 3)
+    row_band = row_band.reshape(NB // GROUP, OUT_ROWS, GROUP * SIDE)
+    stacked = filter_tiles(mix, got_tiles, col_band, row_band)
+
+    parts = lax.all_to_all(stacked, "z", split_axis=0, concat_axis=0, tiled=True)
+    parts = parts.reshape(depth, share, OUT_ROWS, SIDE)
+    summed = jnp.sum(parts.astype(jnp.float32), axis=0).astype(jnp.bfloat16)
+
+    def to_owner(values, shift):
+        pairs = []
+        for v in range(visits):
+            for q in range(depth):
+                for c in range(cores):
+                    target = v * cores + c + shift
+                    if 0 <= target < owners:
+                        pairs.append(((v * depth + q) * cores + c, q * owners + target))
+        return lax.ppermute(values, every, pairs).astype(jnp.float32)
+
+    center = to_owner(summed[:, TOP : TOP + SIDE], 0)
+    lower = to_owner(summed[:, TOP - HALF : TOP], -1)
+    upper = to_owner(summed[:, TOP + SIDE : TOP + SIDE + HALF], 1)
+    rest = ((0, 0), (0, SIDE - HALF), (0, 0))
+    numerator = center + jnp.pad(upper, rest)
+    numerator = numerator + jnp.pad(lower, ((0, 0), (SIDE - HALF, 0), (0, 0)))
+    return (numerator / (1.0 + own_weight)[:, None, None])[None]
+
+
 def solution(mesh):
+    visits, rafts = mesh.shape["visit"], mesh.shape["raft"]
+    cores = 2
+    if visits * cores == rafts and PATCH_DEV % visits == 0:
+        depth = rafts // cores
+        split = Mesh(mesh.devices.reshape(visits, depth, cores), ("visit", "z", "core"))
+        every = ("visit", "z", "core")
+        placed = (P(every, None), P(every), P(every, None), P(every, None), P(every), P(), P())
+        return jax.shard_map(
+            functools.partial(plane_body, visits, depth, cores),
+            mesh=split,
+            in_specs=placed,
+            out_specs=P(("z", "core"), "visit", None, None),
+            check_vma=False,
+        )
     placed = (
         P(("visit", "raft"), None),
         P(("visit", "raft")),

time: 368 us -> 205 us (0.56)
  waiting for transfers between devices: 197 us -> 72.5 us
  local copies, waits for them, and re-layouts: 61.9 us -> 4.15 us
  matrix products: 63.7 us -> 7.8 us
  Pallas kernels: 0 us -> 41.3 us
  blocking collectives: 6.16 us -> 46 us
  between operations: 14.2 us -> 0.15 us
  starting transfers between devices: 16.1 us -> 24.8 us
    all_to_all x2 -> x3, waiting for transfers between devices: 142 us -> 62.8 us  [the longest x1 62.8 us: plane_body(): lax.all_to_all(send_tiles, plane, split_axis=0, concat_axis=0, tiled=True)]
    dot_general x5 -> x2, matrix products: 60 us -> 5.28 us  [the longest x1 4.44 us: plane_body(): jnp.dot(placing, tiles, preferred_element_type=jnp.float32)]
    psum x0 -> x1, blocking collectives: none -> 46 us  [plane_body(): weight_total = lax.psum(weight_sum, every)]
    pallas_call x0 -> x1, Pallas kernels: none -> 41.3 us  [filter_tiles(): pl.pallas_call(filter_kernel, grid=(steps,), out_shape=jax.ShapeDtypeStru...]
    reshape x1, local copies, waits for them, and re-layouts: 28.3 us -> 1.23 us  [plane_body(): row_band = row_band.reshape(NB // GROUP, OUT_ROWS, GROUP * SIDE)]
    ppermute x2 -> x3, waiting for transfers between devices: 32.6 us -> 9.68 us  [to_owner(): return lax.ppermute(values, every, pairs).astype(jnp.float32)]
    reduce_scatter x1 -> x0, waiting for transfers between devices: 22.6 us -> none  [body(): lax.psum_scatter(stacked, 'visit', scatter_dimension=0, tiled=True)]
    unnamed x12 -> x10, local copies, waits for them, and re-layouts: 16.3 us -> 0.19 us
  transfers between devices with their start and end apart: 5 -> 6, of which waited for: 5 -> 2; matrix products, arithmetic and copies ran while one was open for 3% -> 6% of each run, Pallas kernels for 0% -> 0%
where the time goes in v1:
time: 205 us; the launch traced here: 204 us
  waiting for transfers between devices  72.5 us (35%)
  blocking collectives  46 us (22%)
  Pallas kernels  41.3 us (20%)
  starting transfers between devices  24.8 us (12%)
  matrix products  7.8 us (4%)
  other arithmetic  7.24 us (4%)
  local copies, waits for them, and re-layouts  4.15 us (2%)
    all_to_all x1, waiting for transfers between devices, plane_body(): lax.all_to_all(send_tiles, plane, split_axis=0, concat_axis=0, tiled=True)  62.8 us
    psum x1, blocking collectives, plane_body(): weight_total = lax.psum(weight_sum, every)  46 us
    pallas_call x1, Pallas kernels, filter_tiles(): pl.pallas_call(filter_kernel, grid=(steps,), out_shape=jax.ShapeDtypeStru...  41.3 us
    ppermute x3, starting transfers between devices, to_owner(): return lax.ppermute(values, every, pairs).astype(jnp.float32)  10.4 us
    ppermute x3, waiting for transfers between devices, to_owner(): return lax.ppermute(values, every, pairs).astype(jnp.float32)  9.68 us
    all_to_all x1, starting transfers between devices, plane_body(): lax.all_to_all(send_tiles, plane, split_axis=0, concat_axis=0, tiled=True)  5.24 us
    all_to_all x1, starting transfers between devices, plane_body(): lax.all_to_all(stacked, 'z', split_axis=0, concat_axis=0, tiled=True)  4.6 us
    all_to_all x1, starting transfers between devices, plane_body(): lax.all_to_all(send_terms, plane, split_axis=0, concat_axis=0, tiled=True)  4.57 us
  transfers between devices with their start and end apart: 6, of which 2 were waited for; matrix products, arithmetic and copies ran while one was open for 6% of the time, Pallas kernels for 0%

profile of v1, /device:TPU:3, one launch (start us, length us, event | category | flops | bytes accessed | tf_op | source)
XLA Modules:
  0.0 203.9 jit_solution(15122410959594566027)
XLA Ops:
  0.0 0.0 copy-start
  0.0 0.9 fusion.9
  0.9 0.1 reduce_window_sum.11
  1.0 0.8 select_reduce_fusion.1
  1.9 0.7 fusion.10
  2.6 0.7 multiply_add_fusion
  3.3 0.7 multiply_convert_fusion
  4.0 0.1 copy.19
  4.1 0.1 pad.20.clone
  4.2 0.8 convolution_convert_fusion.1
  5.1 4.6 %all-to-all-start = ((bf16[8,24,128]{2,1,0:T(8,128)(2,1)}), bf16[8,24,128]{2,1,0:T(8,128)(2,1)S(1)}, u32[]{:S(2)}, u32[]{:S(2)}) async-start(bf16[8,24,128]{2,1,0:T(8,128)(2,1)} %bitcast.1), calls=%async_computation | async-start | bytes 98304 | tf_op jit(solution)/shard_map/all_to_all | solution.py:202
  9.6 0.0 copy-done
  9.6 4.4 %convolution_convert_fusion = bf16[192,16384]{1,0:T(8,128)(2,1)} fusion(bf16[96,16384]{1,0:T(8,128)(2,1)S(1)} %copy-done, s32[96]{0:T(128)S(1)} %get-tuple-element.8), kind=kOutput, calls=%fused_computation | convolution fusion | flops 607143936 | bytes 9437568 | tf_op jit(solution)/shard_map/dot_general | solution.py:200
  14.1 0.0 all-to-all-done
  14.1 0.0 copy-start.1
  14.1 5.2 %all-to-all-start.1 = ((bf16[8,24,16384]{2,1,0:T(8,128)(2,1)}), bf16[8,24,16384]{2,1,0:T(8,128)(2,1)}, u32[]{:S(2)}, u32[]{:S(2)}) async-start(bf16[8,24,16384]{2,1,0:T(8,128)(2,1)} %bitcast.33), calls=%async_computation.1 | async-start | bytes 12582912 | tf_op jit(solution)/shard_map/all_to_all | solution.py:203
  19.3 0.0 copy-done.1
  19.4 0.0 copy-start.2
  19.4 1.5 fusion
  20.9 1.9 copy.32
  22.8 0.0 copy-done.2
  22.8 1.0 fusion.6
  23.9 0.5 copy.23
  24.4 1.2 copy.33
  25.6 0.1 slice.21
  25.7 0.1 copy.26
  25.7 0.1 copy.25
  25.8 0.8 broadcast_multiply_fusion
  26.6 62.8 %all-to-all-done.1 = bf16[8,24,16384]{2,1,0:T(8,128)(2,1)} async-done(((bf16[8,24,16384]{2,1,0:T(8,128)(2,1)}), bf16[8,24,16384]{2,1,0:T(8,128)(2,1)}, u32[]{:S(2)}, u32[]{:S(2)}) %all-to-all-start.1) | async-done | bytes 6291488 | tf_op jit(solution)/shard_map/all_to_all | solution.py:203
  89.4 0.0 copy-start.3
  89.4 41.3 %shard_map.73 = bf16[24,176,128]{2,1,0:T(8,128)(2,1)} custom-call(bf16[648,192]{1,0:T(8,128)(2,1)} %bitcast.39, bf16[192,16384]{1,0:T(8,128)(2,1)} %bitcast.7.got_ref, bf16[27,256,128]{2,1,0:T(8,128)(2,1)} %bitcast.35, bf16[3,176,1152]{2,1,0:T(8,128)(2,1)} %bitcast.36), custom_call_target="tpu_custom_call" | custom-call | flops 30000001024 | bytes 10000000 | tf_op jit(solution)/shard_map/pallas_call | solution.py:150
  130.7 4.6 %all-to-all-start.2 = ((bf16[24,176,128]{2,1,0:T(8,128)(2,1)}), bf16[24,176,128]{2,1,0:T(8,128)(2,1)}, u32[]{:S(2)}, u32[]{:S(2)}) async-start(bf16[24,176,128]{2,1,0:T(8,128)(2,1)} %shard_map.73), calls=%async_computation.2 | async-start | bytes 2162688 | tf_op jit(solution)/shard_map/all_to_all | solution.py:217
  135.3 0.0 copy-done.3
  135.3 0.1 select_reduce_fusion
  135.4 46.0 %psum.7 = f32[192]{0:T(256)S(1)} all-reduce(f32[192]{0:T(256)S(1)} %select_reduce_fusion), channel_id=1, replica_groups=mesh['visit'=4,'z'=4,'core'=2] {'visit','z','core'}, use_global_device_ids=true, to_apply=%region_4.5 | all-reduce | flops 192 | bytes 1536 | tf_op jit(solution)/shard_map/psum | solution.py:184
  181.4 0.0 all-to-all-done.2
  181.4 1.4 reduce_sum.31
  182.9 1.9 collective-permute-start
  184.8 6.6 %collective-permute-start.1 = (bf16[6,20,128]{2,1,0:T(8,128)(2,1)S(1)}, bf16[6,20,128]{2,1,0:T(8,128)(2,1)S(1)}, u32[]{:S(2)}, u32[]{:S(2)}) collective-permute-start(bf16[6,20,128]{2,1,0:T(8,128)(2,1)S(1)} %get-tuple-element.5), channel_id=1, source_target_pairs={{0,1},{1,2},{2,9},{3,10},{4,17},{5,18},{6,25},{7,26},{8,3},{9,4},{... | collective-permute-start | bytes 92168 | tf_op jit(solution)/shard_map/ppermute | solution.py:229
  191.4 1.9 collective-permute-start.2
  193.3 0.1 dynamic-slice_add_fusion
  193.4 9.7 %collective-permute-done.1 = bf16[6,20,128]{2,1,0:T(8,128)(2,1)S(1)} collective-permute-done((bf16[6,20,128]{2,1,0:T(8,128)(2,1)S(1)}, bf16[6,20,128]{2,1,0:T(8,128)(2,1)S(1)}, u32[]{:S(2)}, u32[]{:S(2)}) %collective-permute-start.1) | collective-permute-done | bytes 30752 | tf_op jit(solution)/shard_map/ppermute | solution.py:229
  203.1 0.0 collective-permute-done.2
  203.1 0.0 collective-permute-done
  203.1 0.8 divide_bitcast_fusion
  (6 shorter events, 0.1 us)
Async XLA Ops:
  0.0 9.6 %copy-start = (bf16[96,16384]{1,0:T(8,128)(2,1)S(1)}, bf16[96,16384]{1,0:T(8,128)(2,1)}, u32[]{:S(2)}) copy-start(bf16[96,16384]{1,0:T(8,128)(2,1)} %param.7) | copy-start | bytes 9437188
  5.1 9.0 %all-to-all-start = ((bf16[8,24,128]{2,1,0:T(8,128)(2,1)}), bf16[8,24,128]{2,1,0:T(8,128)(2,1)S(1)}, u32[]{:S(2)}, u32[]{:S(2)}) async-start(bf16[8,24,128]{2,1,0:T(8,128)(2,1)} %bitcast.1), calls=%async_computation | async-start | bytes 98304 | tf_op jit(solution)/shard_map/all_to_all | solution.py:202
  14.1 5.3 %copy-start.1 = (bf16[27,41]{1,0:T(8,128)(2,1)S(1)}, bf16[27,41]{1,0:T(8,128)(2,1)}, u32[]{:S(2)}) copy-start(bf16[27,41]{1,0:T(8,128)(2,1)} %param.13) | copy-start | bytes 6646
  14.1 75.4 %all-to-all-start.1 = ((bf16[8,24,16384]{2,1,0:T(8,128)(2,1)}), bf16[8,24,16384]{2,1,0:T(8,128)(2,1)}, u32[]{:S(2)}, u32[]{:S(2)}) async-start(bf16[8,24,16384]{2,1,0:T(8,128)(2,1)} %bitcast.33), calls=%async_computation.1 | async-start | bytes 12582912 | tf_op jit(solution)/shard_map/all_to_all | solution.py:203
  19.4 3.5 %copy-start.2 = (bf16[27,41]{1,0:T(8,128)(2,1)S(1)}, bf16[27,41]{1,0:T(8,128)(2,1)}, u32[]{:S(2)}) copy-start(bf16[27,41]{1,0:T(8,128)(2,1)} %param.12) | copy-start | bytes 6646
  89.4 45.9 %copy-start.3 = (f32[96]{0:T(128)S(1)}, f32[96]{0:T(128)}, u32[]{:S(2)}) copy-start(f32[96]{0:T(128)} %param.8) | copy-start | bytes 1156
  130.7 50.7 %all-to-all-start.2 = ((bf16[24,176,128]{2,1,0:T(8,128)(2,1)}), bf16[24,176,128]{2,1,0:T(8,128)(2,1)}, u32[]{:S(2)}, u32[]{:S(2)}) async-start(bf16[24,176,128]{2,1,0:T(8,128)(2,1)} %shard_map.73), calls=%async_computation.2 | async-start | bytes 2162688 | tf_op jit(solution)/shard_map/all_to_all | solution.py:217
  182.9 20.2 %collective-permute-start = (bf16[6,128,128]{2,1,0:T(8,128)(2,1)S(1)}, bf16[6,128,128]{2,1,0:T(8,128)(2,1)S(1)}, u32[]{:S(2)}, u32[]{:S(2)}) collective-permute-start(bf16[6,128,128]{2,1,0:T(8,128)(2,1)S(1)} %slice.22), channel_id=1, source_target_pairs={{0,0},{1,1},{2,8},{3,9},{4,16},{5,17},{6,24},{7,25},{8,2},{9,3},{1... | collective-permute-start | bytes 589832 | tf_op jit(solution)/shard_map/ppermute | solution.py:229
  184.8 18.3 %collective-permute-start.1 = (bf16[6,20,128]{2,1,0:T(8,128)(2,1)S(1)}, bf16[6,20,128]{2,1,0:T(8,128)(2,1)S(1)}, u32[]{:S(2)}, u32[]{:S(2)}) collective-permute-start(bf16[6,20,128]{2,1,0:T(8,128)(2,1)S(1)} %get-tuple-element.5), channel_id=1, source_target_pairs={{0,1},{1,2},{2,9},{3,10},{4,17},{5,18},{6,25},{7,26},{8,3},{9,4},{... | collective-permute-start | bytes 92168 | tf_op jit(solution)/shard_map/ppermute | solution.py:229
  191.4 11.7 %collective-permute-start.2 = (bf16[6,20,128]{2,1,0:T(8,128)(2,1)S(1)}, bf16[6,20,128]{2,1,0:T(8,128)(2,1)S(1)}, u32[]{:S(2)}, u32[]{:S(2)}) collective-permute-start(bf16[6,20,128]{2,1,0:T(8,128)(2,1)S(1)} %get-tuple-element.6), channel_id=1, source_target_pairs={{1,0},{3,8},{5,16},{7,24},{8,1},{9,2},{10,9},{11,10},{12,17},{13,1... | collective-permute-start | bytes 92168 | tf_op jit(solution)/shard_map/ppermute | solution.py:229

commit v2 on v1

--- a/solution.py
+++ b/solution.py
@@ -15,6 +15,7 @@
 HALF = (KERNEL - 1) // 2
 TOP = 24
 OUT_ROWS = 176
+FIRST = 80
 
 
 def with_halo(shard, sides, width):
@@ -91,10 +92,13 @@
     return coadd_image[None]
 
 
-def filter_kernel(mix_ref, got_ref, col_ref, row_ref, out_ref, planes, strip, filtered, total):
+def filter_kernel(final, lines, mix_ref, got_ref, col_ref, row_ref, *rest):
+    if final:
+        before_ref, weight_ref, out_ref, planes, strip, filtered, total = rest
+    else:
+        total, planes, strip, filtered = rest
     step = pl.program_id(0)
     count = GROUP * PATCH_DEV
-    lines = got_ref.shape[1] // SIDE
     blocks = PATCH_DEV + 1
 
     def make_planes(pair, carry):
@@ -111,19 +115,25 @@
 
     @pl.when(step == 0)
     def _():
-        strip[:, :SIDE] = jnp.zeros((lines, SIDE), jnp.bfloat16)
-        strip[:, (PATCH_DEV + 1) * SIDE :] = jnp.zeros((lines, SIDE), jnp.bfloat16)
+        strip[:lines, :SIDE] = jnp.zeros((lines, SIDE), jnp.bfloat16)
+        strip[PATCH_DEV * lines :, SIDE:] = jnp.zeros((lines, SIDE), jnp.bfloat16)
 
     def filter_columns(basis, carry):
         for place in range(PATCH_DEV):
             image = planes[pl.ds(basis * PATCH_DEV + place, lines, stride=count), :]
-            strip[:, (place + 1) * SIDE : (place + 2) * SIDE] = image.astype(jnp.bfloat16)
+            image = image.astype(jnp.bfloat16)
+            strip[place * lines : (place + 1) * lines, SIDE:] = image
+            strip[(place + 1) * lines : (place + 2) * lines, :SIDE] = image
         rows = pl.ds(pl.multiple_of(basis * lines, 16), lines)
-        for block in range(blocks):
-            wide = strip[:, block * SIDE : (block + 2) * SIDE]
-            filtered[rows, block * SIDE : (block + 1) * SIDE] = jnp.dot(
-                wide, col_ref[basis], preferred_element_type=jnp.float32
+        for first in range(0, blocks, 5):
+            wide = jnp.dot(
+                strip[first * lines : (first + 5) * lines, :],
+                col_ref[basis],
+                preferred_element_type=jnp.float32,
             ).astype(jnp.bfloat16)
+            for block in range(5):
+                low = (first + block) * SIDE
+                filtered[rows, low : low + SIDE] = wide[block * lines : (block + 1) * lines]
         return carry
 
     lax.fori_loop(0, GROUP, filter_columns, 0)
@@ -132,43 +142,59 @@
     for chunk in range(blocks // 5):
         span = slice(chunk * width, (chunk + 1) * width)
         part = jnp.dot(row_ref[0], filtered[:, span], preferred_element_type=jnp.float32)
-        total[:, span] = jnp.where(step == 0, part, total[:, span] + part)
-
-    @pl.when(step == NB // GROUP - 1)
-    def _():
-        for place in range(PATCH_DEV):
-            low = place * SIDE + SIDE // 2
-            out_ref[place] = total[:, low : low + SIDE].astype(jnp.bfloat16)
-
-
-def filter_tiles(mix, got, col_band, row_band):
+        start = before_ref[:, span] if final else 0.0
+        total[:, span] = part + jnp.where(step == 0, start, total[:, span])
+
+    if final:
+
+        @pl.when(step == NB // GROUP - 1)
+        def _():
+            for place in range(PATCH_DEV):
+                low = place * SIDE + SIDE // 2
+                image = total[:, low : low + SIDE]
+                out_ref[place, :16] = (image[:16] + weight_ref[place]).astype(jnp.bfloat16)
+                out_ref[place, 16:] = image[16:].astype(jnp.bfloat16)
+
+
+def filter_tiles(lines, mix, got, col_band, row_band, before=None, weight=None):
     slots, pixels = got.shape
-    lines = pixels // SIDE
     steps = NB // GROUP
     count = GROUP * PATCH_DEV
-    width = (PATCH_DEV + 1) * SIDE
+    blocks = PATCH_DEV + 1
+    final = before is not None
+    args = [mix, got, col_band, row_band]
+    in_specs = [
+        pl.BlockSpec((count, slots), lambda s: (s, 0)),
+        pl.BlockSpec((slots, pixels), lambda s: (0, 0)),
+        pl.BlockSpec((GROUP, 2 * SIDE, SIDE), lambda s: (s, 0, 0)),
+        pl.BlockSpec((1, OUT_ROWS, GROUP * lines), lambda s: (s, 0, 0)),
+    ]
+    whole = pl.BlockSpec((OUT_ROWS, blocks * SIDE), lambda s: (0, 0))
+    scratch = [
+        pltpu.VMEM((lines * count, SIDE), jnp.float32),
+        pltpu.VMEM((blocks * lines, 2 * SIDE), jnp.bfloat16),
+        pltpu.VMEM((GROUP * lines, blocks * SIDE), jnp.bfloat16),
+    ]
+    out_shape = jax.ShapeDtypeStruct((OUT_ROWS, blocks * SIDE), jnp.float32)
+    out_specs = whole
+    if final:
+        args += [before, weight]
+        in_specs += [whole, pl.BlockSpec((PATCH_DEV, 16, SIDE), lambda s: (0, 0, 0))]
+        scratch += [pltpu.VMEM((OUT_ROWS, blocks * SIDE), jnp.float32)]
+        out_shape = jax.ShapeDtypeStruct((PATCH_DEV, OUT_ROWS, SIDE), jnp.bfloat16)
+        out_specs = pl.BlockSpec((PATCH_DEV, OUT_ROWS, SIDE), lambda s: (0, 0, 0))
     return pl.pallas_call(
-        filter_kernel,
+        functools.partial(filter_kernel, final, lines),
         grid=(steps,),
-        out_shape=jax.ShapeDtypeStruct((PATCH_DEV, OUT_ROWS, SIDE), jnp.bfloat16),
-        in_specs=[
-            pl.BlockSpec((count, slots), lambda s: (s, 0)),
-            pl.BlockSpec((slots, pixels), lambda s: (0, 0)),
-            pl.BlockSpec((GROUP, 2 * SIDE, SIDE), lambda s: (s, 0, 0)),
-            pl.BlockSpec((1, OUT_ROWS, GROUP * lines), lambda s: (s, 0, 0)),
-        ],
-        out_specs=pl.BlockSpec((PATCH_DEV, OUT_ROWS, SIDE), lambda s: (0, 0, 0)),
-        scratch_shapes=[
-            pltpu.VMEM((lines * count, SIDE), jnp.float32),
-            pltpu.VMEM((lines, (PATCH_DEV + 2) * SIDE), jnp.bfloat16),
-            pltpu.VMEM((GROUP * lines, width), jnp.bfloat16),
-            pltpu.VMEM((OUT_ROWS, width), jnp.float32),
-        ],
+        out_shape=out_shape,
+        in_specs=in_specs,
+        out_specs=out_specs,
+        scratch_shapes=scratch,
         compiler_params=pltpu.CompilerParams(vmem_limit_bytes=56 * 1024 * 1024),
         cost_estimate=pl.CostEstimate(
-            flops=30_000_000_000, bytes_accessed=10_000_000, transcendentals=0
+            flops=200_000_000 * lines, bytes_accessed=100_000 * lines, transcendentals=0
         ),
-    )(mix, got, col_band, row_band)
+    )(*args)
 
 
 def plane_body(visits, depth, cores, tiles, weights, coef, owner, patch, row_taps, col_taps):
@@ -177,33 +203,39 @@
     capacity = 2 * tile_count // owners
     every = ("visit", "z", "core")
     owner_ids = owner[:, 0]
-    plain_weight = weights.astype(jnp.bfloat16).astype(jnp.float32)
-    keys = owner_ids * PATCH_DEV + patch
-    key_hits = keys[:, None] == jnp.arange(owners * PATCH_DEV)[None, :]
-    weight_sum = jnp.sum(jnp.where(key_hits, plain_weight[:, None], 0.0), axis=0)
-    weight_total = lax.psum(weight_sum, every)
-    strip_id = lax.axis_index("z") * cores + lax.axis_index("core")
     share = PATCH_DEV // visits
-    own_weight = lax.dynamic_slice(
-        weight_total, (strip_id * PATCH_DEV + lax.axis_index("visit") * share,), (share,)
-    )
-
+    plain_weight = weights.astype(jnp.bfloat16)[:, None]
     owner_hits = (owner_ids[:, None] == jnp.arange(owners)[None, :]).astype(jnp.int32)
     slot_rank = jnp.sum(jnp.cumsum(owner_hits, axis=0) * owner_hits, axis=1) - 1
     slot_index = owner_ids * capacity + slot_rank
     placing = (jnp.arange(owners * capacity)[:, None] == slot_index[None, :]).astype(jnp.bfloat16)
     scaled = (weights[:, None] * coef).astype(jnp.bfloat16)
     patch_hits = (patch[:, None] == jnp.arange(PATCH_DEV)[None, :]).astype(jnp.bfloat16)
-    blank = jnp.zeros((tile_count, SIDE - NB - PATCH_DEV), jnp.bfloat16)
-    terms = jnp.concatenate([scaled, patch_hits, blank], axis=1)
-    send_terms = jnp.dot(placing, terms, preferred_element_type=jnp.float32).astype(jnp.bfloat16)
-    send_tiles = jnp.dot(placing, tiles, preferred_element_type=jnp.float32).astype(jnp.bfloat16)
-    plane = ("visit", "core")
-    got_terms = lax.all_to_all(send_terms, plane, split_axis=0, concat_axis=0, tiled=True)
-    got_tiles = lax.all_to_all(send_tiles, plane, split_axis=0, concat_axis=0, tiled=True)
+    blank = jnp.zeros((tile_count, SIDE - NB - PATCH_DEV - 1), jnp.bfloat16)
+    terms = jnp.concatenate([scaled, patch_hits, plain_weight, blank], axis=1)
+
+    def place(values):
+        return jnp.dot(placing, values, preferred_element_type=jnp.float32).astype(jnp.bfloat16)
+
+    def exchange(values):
+        return lax.all_to_all(
+            values, ("visit", "core"), split_axis=0, concat_axis=0, tiled=True
+        )
+
+    cut = FIRST * SIDE
+    got_first = exchange(place(jnp.concatenate([tiles[:, :cut], terms], axis=1)))
+    got_first, held = lax.optimization_barrier((got_first, place(tiles[:, cut:])))
+    got_second = exchange(held)
+    got_terms = got_first[:, cut:]
     by_basis = got_terms[:, :NB].T
-    by_patch = got_terms[:, NB : NB + PATCH_DEV].T
-    mix = (by_basis[:, None, :] * by_patch[None, :, :]).reshape(NB * PATCH_DEV, -1)
+    hits = got_terms[:, NB : NB + PATCH_DEV]
+    mix = (by_basis[:, None, :] * hits.T[None, :, :]).reshape(NB * PATCH_DEV, -1)
+    got_weight = got_terms[:, NB + PATCH_DEV :][:, :1].astype(jnp.float32)
+    weight_sum = jnp.sum(got_weight * hits.astype(jnp.float32), axis=0)
+    high = lax.reduce_precision(weight_sum, 8, 7)
+    halves = jnp.stack([high, weight_sum - high], axis=1)
+    weight_rows = jnp.pad(halves, ((0, 0), (0, 14)))[:, :, None]
+    weight_rows = jnp.broadcast_to(weight_rows, (PATCH_DEV, 16, SIDE))
 
     wide_index = jnp.arange(2 * SIDE)
     narrow = jnp.arange(SIDE)
@@ -211,12 +243,17 @@
     out_index = jnp.arange(OUT_ROWS)
     row_band = tap_band(row_taps, narrow[None, :] - out_index[:, None] + TOP + HALF)
     row_band = row_band.reshape(NB // GROUP, GROUP, OUT_ROWS, SIDE).transpose(0, 2, 1, 3)
-    row_band = row_band.reshape(NB // GROUP, OUT_ROWS, GROUP * SIDE)
-    stacked = filter_tiles(mix, got_tiles, col_band, row_band)
+    row_first = row_band[..., :FIRST].reshape(NB // GROUP, OUT_ROWS, -1)
+    row_second = row_band[..., FIRST:].reshape(NB // GROUP, OUT_ROWS, -1)
+    partial = filter_tiles(FIRST, mix, got_first, col_band, row_first)
+    stacked = filter_tiles(
+        SIDE - FIRST, mix, got_second, col_band, row_second, partial, weight_rows
+    )
 
     parts = lax.all_to_all(stacked, "z", split_axis=0, concat_axis=0, tiled=True)
-    parts = parts.reshape(depth, share, OUT_ROWS, SIDE)
-    summed = jnp.sum(parts.astype(jnp.float32), axis=0).astype(jnp.bfloat16)
+    parts = parts.reshape(depth, share, OUT_ROWS, SIDE).astype(jnp.float32)
+    summed = jnp.sum(parts, axis=0).astype(jnp.bfloat16)
+    plane_weight = jnp.sum(parts[:, :, :2], axis=(0, 2))
 
     def to_owner(values, shift):
         pairs = []
@@ -231,10 +268,11 @@
     center = to_owner(summed[:, TOP : TOP + SIDE], 0)
     lower = to_owner(summed[:, TOP - HALF : TOP], -1)
     upper = to_owner(summed[:, TOP + SIDE : TOP + SIDE + HALF], 1)
+    own_weight = to_owner(plane_weight, 0)
     rest = ((0, 0), (0, SIDE - HALF), (0, 0))
     numerator = center + jnp.pad(upper, rest)
     numerator = numerator + jnp.pad(lower, ((0, 0), (SIDE - HALF, 0), (0, 0)))
-    return (numerator / (1.0 + own_weight)[:, None, None])[None]
+    return (numerator / (1.0 + own_weight)[:, None, :])[None]
 
 
 def solution(mesh):

time: 205 us -> 180 us (0.88)
  waiting for transfers between devices: 72.5 us -> 41.3 us
  blocking collectives: 46 us -> 31.3 us
  local copies, waits for them, and re-layouts: 4.15 us -> 16.8 us
  Pallas kernels: 41.3 us -> 52.7 us
  other arithmetic: 7.24 us -> 4.2 us
  starting transfers between devices: 24.8 us -> 21.8 us
    psum x1 -> x0, blocking collectives: 46 us -> none  [plane_body(): weight_total = lax.psum(weight_sum, every)]
    all_to_all x3 -> x2, waiting for transfers between devices: 62.8 us -> 31.5 us  [exchange(): lax.all_to_all(values, ('visit', 'core'), split_axis=0, concat_axis=0, ti...]
    all_to_all x0 -> x1, blocking collectives: none -> 31.3 us  [plane_body(): lax.all_to_all(stacked, 'z', split_axis=0, concat_axis=0, tiled=True)]
    pallas_call x1 -> x2, Pallas kernels: 41.3 us -> 52.7 us  [filter_tiles(): pl.pallas_call(functools.partial(filter_kernel, final, lines), grid=(step...]
    slice x1 -> x4, local copies, waits for them, and re-layouts: 0.08 us -> 5.69 us  [the longest x1 3 us: plane_body(): tiles[:, :cut]]
    all_to_all x3 -> x2, starting transfers between devices: 14.4 us -> 9.73 us  [exchange(): lax.all_to_all(values, ('visit', 'core'), split_axis=0, concat_axis=0, ti...]
    concatenate x1, local copies, waits for them, and re-layouts: 0.08 us -> 2.45 us  [plane_body(): jnp.concatenate([tiles[:, :cut], terms], axis=1)]
    ppermute x3 -> x4, starting transfers between devices: 10.4 us -> 12.1 us  [to_owner(): return lax.ppermute(values, every, pairs).astype(jnp.float32)]
  transfers between devices with their start and end apart: 6 -> 6, of which waited for: 2 -> 2; matrix products, arithmetic and copies ran while one was open for 6% -> 9% of each run, Pallas kernels for 0% -> 17%
where the time goes in v2:
time: 180 us; the launch traced here: 177 us
  Pallas kernels  52.7 us (29%)
  waiting for transfers between devices  41.3 us (23%)
  blocking collectives  31.3 us (17%)
  starting transfers between devices  21.8 us (12%)
  local copies, waits for them, and re-layouts  16.8 us (9%)
  matrix products  9.1 us (5%)
  other arithmetic  4.2 us (2%)
    pallas_call x2, Pallas kernels, filter_tiles(): pl.pallas_call(functools.partial(filter_kernel, final, lines), grid=(step...  52.7 us
    all_to_all x2, waiting for transfers between devices, exchange(): lax.all_to_all(values, ('visit', 'core'), split_axis=0, concat_axis=0, ti...  31.5 us
    all_to_all x1, blocking collectives, plane_body(): lax.all_to_all(stacked, 'z', split_axis=0, concat_axis=0, tiled=True)  31.3 us
    ppermute x4, starting transfers between devices, to_owner(): return lax.ppermute(values, every, pairs).astype(jnp.float32)  12.1 us
    all_to_all x2, starting transfers between devices, exchange(): lax.all_to_all(values, ('visit', 'core'), split_axis=0, concat_axis=0, ti...  9.73 us
    ppermute x4, waiting for transfers between devices, to_owner(): return lax.ppermute(values, every, pairs).astype(jnp.float32)  9.71 us
    dot_general x2, matrix products, place(): jnp.dot(placing, values, preferred_element_type=jnp.float32)  6.58 us
  transfers between devices with their start and end apart: 6, of which 2 were waited for; matrix products, arithmetic and copies ran while one was open for 9% of the time, Pallas kernels for 17%

profile of v2, /device:TPU:3, one launch (start us, length us, event | category | flops | bytes accessed | tf_op | source)
XLA Modules:
  0.0 177.4 jit_solution(3404923163702310772)
XLA Ops:
  0.0 0.0 copy-start
  0.0 0.0 copy-start.5
  0.0 0.0 copy-start.2
  0.0 0.0 copy-start.6
  0.0 0.0 copy-start.4
  0.0 3.0 %slice.42 = bf16[96,10240]{1,0:T(8,128)(2,1)} slice(bf16[96,16384]{1,0:T(8,128)(2,1)} %param.7), slice={[0:96], [0:10240]} | slice | bytes 3932160 | tf_op jit(solution)/shard_map/slice | solution.py:226
  3.0 0.0 copy-done.5
  3.0 0.0 copy-done.2
  3.1 0.1 copy.15
  3.2 0.0 copy-done.6
  3.2 0.1 fusion.11
  3.3 0.1 copy.16
  3.4 0.0 copy-done.4
  3.4 0.1 fusion.10
  3.5 0.1 reduce_window_sum.11
  3.6 0.2 select_reduce_fusion
  3.8 2.5 %concatenate.3 = bf16[96,10368]{1,0:T(8,128)(2,1)S(1)} concatenate(bf16[96,10240]{1,0:T(8,128)(2,1)} %slice.42, bf16[96,27]{1,0:T(8,128)(2,1)S(1)} %copy.15, bf16[96,24]{1,0:T(8,128)(2,1)S(1)} %fusion.11, bf16[96,1]{1,0:T(8,128)(2,1)S(1)} %copy.16, bf16[96,76]{1,0:T(8,128)(2,1)S(1)} %broadcast_in_dim.9), dimensions={1} | concatenate | bytes 3981312 | tf_op jit(solution)/shard_map/concatenate | solution.py:226
  6.3 3.1 %convolution_convert_fusion = bf16[192,10368]{1,0:T(8,128)(2,1)} fusion(bf16[96,10368]{1,0:T(8,128)(2,1)S(1)} %concatenate.3, s32[96]{0:T(128)S(1)} %add_add_fusion), kind=kOutput, calls=%fused_computation | convolution fusion | flops 384215040 | bytes 5972352 | tf_op jit(solution)/shard_map/dot_general | solution.py:218
  9.4 4.6 %all-to-all-start = ((bf16[8,24,10368]{2,1,0:T(8,128)(2,1)}), bf16[8,24,10368]{2,1,0:T(8,128)(2,1)}, u32[]{:S(2)}, u32[]{:S(2)}) async-start(bf16[8,24,10368]{2,1,0:T(8,128)(2,1)} %bitcast.39), calls=%async_computation | async-start | bytes 7962624 | tf_op jit(solution)/shard_map/all_to_all | solution.py:221
  13.9 0.0 copy-done
  14.0 1.5 fusion
  15.4 0.0 copy-start.3
  15.5 1.9 %copy.30 = bf16[256,128,27]{1,0,2:T(8,128)(2,1)} copy(bf16[256,128,27]{1,2,0:T(8,128)(2,1)S(1)} %fusion) | data formatting | bytes 3538944 | tf_op jit(solution)/shard_map/qrj,bj->bqr/dot_general | solution.py:38
  17.4 0.0 copy-done.3
  17.4 1.0 fusion.6
  18.4 0.5 copy.20
  18.9 0.4 slice.54
  19.4 1.1 copy.21
  20.5 1.1 copy.25.row_ref
  21.6 1.2 copy.22
  22.7 1.5 copy.23.row_ref
  24.2 3.5 %convolution_convert_fusion.1 = bf16[192,6144]{1,0:T(8,128)(2,1)} fusion(bf16[96,16384]{1,0:T(8,128)(2,1)} %param.7, s32[96]{0:T(128)S(1)} %add_add_fusion), kind=kOutput, calls=%fused_computation.1 | convolution fusion | flops 227690496 | bytes 3539328 | tf_op jit(solution)/shard_map/dot_general | solution.py:218
  27.7 31.5 %all-to-all-done = bf16[8,24,10368]{2,1,0:T(8,128)(2,1)} async-done(((bf16[8,24,10368]{2,1,0:T(8,128)(2,1)}), bf16[8,24,10368]{2,1,0:T(8,128)(2,1)}, u32[]{:S(2)}, u32[]{:S(2)}) %all-to-all-start) | async-done | bytes 3981344 | tf_op jit(solution)/shard_map/all_to_all | solution.py:221
  59.2 0.9 slice_bitcast_fusion.1
  60.1 0.8 slice_bitcast_fusion
  60.9 1.0 convert_reduce_fusion
  61.9 0.1 copy.18
  62.0 0.1 copy.17
  62.1 5.2 %all-to-all-start.1 = ((bf16[8,24,6144]{2,1,0:T(8,128)(2,1)}), bf16[8,24,6144]{2,1,0:T(8,128)(2,1)S(1)}, u32[]{:S(2)}, u32[]{:S(2)}) async-start(bf16[8,24,6144]{2,1,0:T(8,128)(2,1)} %bitcast.7), calls=%async_computation.1 | async-start | bytes 4718592 | tf_op jit(solution)/shard_map/all_to_all | solution.py:221
  67.3 0.9 multiply_reduce_fusion
  68.2 0.1 copy.26
  68.3 0.8 broadcast_multiply_fusion
  69.0 29.8 %shard_map.73.rest_0_ = f32[176,3200]{1,0:T(8,128)} custom-call(bf16[648,192]{1,0:T(8,128)(2,1)} %bitcast.49, bf16[192,10368]{1,0:T(8,128)(2,1)} %bitcast.3.got_ref, bf16[27,256,128]{2,1,0:T(8,128)(2,1)} %bitcast.47, bf16[3,176,720]{2,1,0:T(8,128)(2,1)} %copy.23.row_ref), custom_call_target="tpu_custom_call" | custom-call | flops 16000000000 | bytes 8000000 | tf_op jit(solution)/shard_map/pallas_call | solution.py:186
  98.8 0.0 all-to-all-done.1
  98.8 0.0 copy-start.1
  98.8 0.9 broadcast_in_dim.10.rest_1_
  99.7 0.6 copy-done.1
  100.3 22.9 %shard_map.74 = bf16[24,176,128]{2,1,0:T(8,128)(2,1)} custom-call(bf16[648,192]{1,0:T(8,128)(2,1)} %bitcast.50, bf16[192,6144]{1,0:T(8,128)(2,1)} %bitcast.46, bf16[27,256,128]{2,1,0:T(8,128)(2,1)} %bitcast.48, bf16[3,176,432]{2,1,0:T(8,128)(2,1)} %copy.25.row_ref, f32[176,3200]{1,0:T(8,128)} %shard_map.73.rest_0_, f32[24,16,128]{2,1,0:T(8,128)} %broadcast_in_dim.10.rest_1_), custom_call_target="tpu_custom_call" | custom-call | flops 9600000000 | bytes 4800000 | tf_op jit(solution)/shard_map/pallas_call | solution.py:186
  123.2 31.3 %all_to_all.28 = bf16[24,176,128]{2,1,0:T(8,128)(2,1)S(1)} all-to-all(bf16[24,176,128]{2,1,0:T(8,128)(2,1)} %shard_map.74), channel_id=1, replica_groups=mesh['visit'=4,'z'=4,'core'=2] {'z'}, dimensions={0} | all-to-all | bytes 2162688 | tf_op jit(solution)/shard_map/all_to_all | solution.py:253
  154.5 0.2 reduce_sum.44
  154.7 1.9 %collective-permute-start.3 = (f32[6,128]{1,0:T(8,128)S(1)}, f32[6,128]{1,0:T(8,128)S(1)}, u32[]{:S(2)}, u32[]{:S(2)}) collective-permute-start(f32[6,128]{1,0:T(8,128)S(1)} %convert_reduce_fusion.1), channel_id=1, source_target_pairs={{0,0},{1,1},{2,8},{3,9},{4,16},{5,17},{6,24},{7,25},{8,2},{9,3},{1... | collective-permute-start | bytes 9224 | tf_op jit(solution)/shard_map/ppermute | solution.py:266
  156.7 4.3 %collective-permute-start = (bf16[6,128,128]{2,1,0:T(8,128)(2,1)S(1)}, bf16[6,128,128]{2,1,0:T(8,128)(2,1)S(1)}, u32[]{:S(2)}, u32[]{:S(2)}) collective-permute-start(bf16[6,128,128]{2,1,0:T(8,128)(2,1)S(1)} %slice.56), channel_id=1, source_target_pairs={{0,0},{1,1},{2,8},{3,9},{4,16},{5,17},{6,24},{7,25},{8,2},{9,3},{1... | collective-permute-start | bytes 589832 | tf_op jit(solution)/shard_map/ppermute | solution.py:266
  161.0 3.7 %collective-permute-start.2 = (bf16[6,20,128]{2,1,0:T(8,128)(2,1)S(1)}, bf16[6,20,128]{2,1,0:T(8,128)(2,1)S(1)}, u32[]{:S(2)}, u32[]{:S(2)}) collective-permute-start(bf16[6,20,128]{2,1,0:T(8,128)(2,1)S(1)} %get-tuple-element.10), channel_id=1, source_target_pairs={{1,0},{3,8},{5,16},{7,24},{8,1},{9,2},{10,9},{11,10},{12,17},{13,1... | collective-permute-start | bytes 92168 | tf_op jit(solution)/shard_map/ppermute | solution.py:266
  164.7 2.2 %collective-permute-start.1 = (bf16[6,20,128]{2,1,0:T(8,128)(2,1)S(1)}, bf16[6,20,128]{2,1,0:T(8,128)(2,1)S(1)}, u32[]{:S(2)}, u32[]{:S(2)}) collective-permute-start(bf16[6,20,128]{2,1,0:T(8,128)(2,1)S(1)} %get-tuple-element.9), channel_id=1, source_target_pairs={{0,1},{1,2},{2,9},{3,10},{4,17},{5,18},{6,25},{7,26},{8,3},{9,4},{... | collective-permute-start | bytes 92168 | tf_op jit(solution)/shard_map/ppermute | solution.py:266
  166.9 0.0 collective-permute-done.3
  166.9 0.0 collective-permute-done.2
  166.9 9.7 %collective-permute-done.1 = bf16[6,20,128]{2,1,0:T(8,128)(2,1)S(1)} collective-permute-done((bf16[6,20,128]{2,1,0:T(8,128)(2,1)S(1)}, bf16[6,20,128]{2,1,0:T(8,128)(2,1)S(1)}, u32[]{:S(2)}, u32[]{:S(2)}) %collective-permute-start.1) | collective-permute-done | bytes 30752 | tf_op jit(solution)/shard_map/ppermute | solution.py:266
  176.6 0.0 collective-permute-done
  176.6 0.8 divide_bitcast_fusion
  (13 shorter events, 0.1 us)
Async XLA Ops:
  0.0 13.9 %copy-start = (bf16[27,41]{1,0:T(8,128)(2,1)S(1)}, bf16[27,41]{1,0:T(8,128)(2,1)}, u32[]{:S(2)}) copy-start(bf16[27,41]{1,0:T(8,128)(2,1)} %param.13) | copy-start | bytes 6646
  0.0 3.0 %copy-start.5 = (f32[96]{0:T(128)S(1)}, f32[96]{0:T(128)}, u32[]{:S(2)}) copy-start(f32[96]{0:T(128)} %param.8) | copy-start | bytes 1156
  0.0 3.0 %copy-start.2 = (f32[96,27]{0,1:T(8,128)S(1)}, f32[96,27]{0,1:T(8,128)}, u32[]{:S(2)}) copy-start(f32[96,27]{0,1:T(8,128)} %param.9) | copy-start | bytes 31108
  0.0 3.2 %copy-start.6 = (s32[96]{0:T(128)S(1)}, s32[96]{0:T(128)}, u32[]{:S(2)}) copy-start(s32[96]{0:T(128)} %param.11) | copy-start | bytes 1156
  0.0 3.4 %copy-start.4 = (s32[96,1]{0,1:T(1,128)S(1)}, s32[96,1]{0,1:T(1,128)}, u32[]{:S(2)}) copy-start(s32[96,1]{0,1:T(1,128)} %param.10) | copy-start | bytes 1156
  9.4 49.9 %all-to-all-start = ((bf16[8,24,10368]{2,1,0:T(8,128)(2,1)}), bf16[8,24,10368]{2,1,0:T(8,128)(2,1)}, u32[]{:S(2)}, u32[]{:S(2)}) async-start(bf16[8,24,10368]{2,1,0:T(8,128)(2,1)} %bitcast.39), calls=%async_computation | async-start | bytes 7962624 | tf_op jit(solution)/shard_map/all_to_all | solution.py:221
  15.4 1.9 %copy-start.3 = (bf16[27,41]{1,0:T(8,128)(2,1)S(1)}, bf16[27,41]{1,0:T(8,128)(2,1)}, u32[]{:S(2)}) copy-start(bf16[27,41]{1,0:T(8,128)(2,1)} %param.12) | copy-start | bytes 6646
  62.1 36.8 %all-to-all-start.1 = ((bf16[8,24,6144]{2,1,0:T(8,128)(2,1)}), bf16[8,24,6144]{2,1,0:T(8,128)(2,1)S(1)}, u32[]{:S(2)}, u32[]{:S(2)}) async-start(bf16[8,24,6144]{2,1,0:T(8,128)(2,1)} %bitcast.7), calls=%async_computation.1 | async-start | bytes 4718592 | tf_op jit(solution)/shard_map/all_to_all | solution.py:221
  98.8 1.5 copy-start.1
  154.7 12.2 %collective-permute-start.3 = (f32[6,128]{1,0:T(8,128)S(1)}, f32[6,128]{1,0:T(8,128)S(1)}, u32[]{:S(2)}, u32[]{:S(2)}) collective-permute-start(f32[6,128]{1,0:T(8,128)S(1)} %convert_reduce_fusion.1), channel_id=1, source_target_pairs={{0,0},{1,1},{2,8},{3,9},{4,16},{5,17},{6,24},{7,25},{8,2},{9,3},{1... | collective-permute-start | bytes 9224 | tf_op jit(solution)/shard_map/ppermute | solution.py:266
  156.7 20.0 %collective-permute-start = (bf16[6,128,128]{2,1,0:T(8,128)(2,1)S(1)}, bf16[6,128,128]{2,1,0:T(8,128)(2,1)S(1)}, u32[]{:S(2)}, u32[]{:S(2)}) collective-permute-start(bf16[6,128,128]{2,1,0:T(8,128)(2,1)S(1)} %slice.56), channel_id=1, source_target_pairs={{0,0},{1,1},{2,8},{3,9},{4,16},{5,17},{6,24},{7,25},{8,2},{9,3},{1... | collective-permute-start | bytes 589832 | tf_op jit(solution)/shard_map/ppermute | solution.py:266
  161.0 6.0 %collective-permute-start.2 = (bf16[6,20,128]{2,1,0:T(8,128)(2,1)S(1)}, bf16[6,20,128]{2,1,0:T(8,128)(2,1)S(1)}, u32[]{:S(2)}, u32[]{:S(2)}) collective-permute-start(bf16[6,20,128]{2,1,0:T(8,128)(2,1)S(1)} %get-tuple-element.10), channel_id=1, source_target_pairs={{1,0},{3,8},{5,16},{7,24},{8,1},{9,2},{10,9},{11,10},{12,17},{13,1... | collective-permute-start | bytes 92168 | tf_op jit(solution)/shard_map/ppermute | solution.py:266
  164.7 11.9 %collective-permute-start.1 = (bf16[6,20,128]{2,1,0:T(8,128)(2,1)S(1)}, bf16[6,20,128]{2,1,0:T(8,128)(2,1)S(1)}, u32[]{:S(2)}, u32[]{:S(2)}) collective-permute-start(bf16[6,20,128]{2,1,0:T(8,128)(2,1)S(1)} %get-tuple-element.9), channel_id=1, source_target_pairs={{0,1},{1,2},{2,9},{3,10},{4,17},{5,18},{6,25},{7,26},{8,3},{9,4},{... | collective-permute-start | bytes 92168 | tf_op jit(solution)/shard_map/ppermute | solution.py:266

commit v3 on v2

--- a/solution.py
+++ b/solution.py
@@ -94,9 +94,9 @@
 
 def filter_kernel(final, lines, mix_ref, got_ref, col_ref, row_ref, *rest):
     if final:
-        before_ref, weight_ref, out_ref, planes, strip, filtered, total = rest
+        before_ref, out_ref, planes, strip, filtered, total = rest
     else:
-        total, planes, strip, filtered = rest
+        weight_ref, out_ref, after_ref, planes, strip, filtered, total = rest
     step = pl.program_id(0)
     count = GROUP * PATCH_DEV
     blocks = PATCH_DEV + 1
@@ -125,15 +125,11 @@
             strip[place * lines : (place + 1) * lines, SIDE:] = image
             strip[(place + 1) * lines : (place + 2) * lines, :SIDE] = image
         rows = pl.ds(pl.multiple_of(basis * lines, 16), lines)
-        for first in range(0, blocks, 5):
-            wide = jnp.dot(
-                strip[first * lines : (first + 5) * lines, :],
-                col_ref[basis],
-                preferred_element_type=jnp.float32,
-            ).astype(jnp.bfloat16)
-            for block in range(5):
-                low = (first + block) * SIDE
-                filtered[rows, low : low + SIDE] = wide[block * lines : (block + 1) * lines]
+        wide = jnp.dot(strip[...], col_ref[basis], preferred_element_type=jnp.float32)
+        wide = wide.astype(jnp.bfloat16)
+        for block in range(blocks):
+            low = block * SIDE
+            filtered[rows, low : low + SIDE] = wide[block * lines : (block + 1) * lines]
         return carry
 
     lax.fori_loop(0, GROUP, filter_columns, 0)
@@ -145,15 +141,55 @@
         start = before_ref[:, span] if final else 0.0
         total[:, span] = part + jnp.where(step == 0, start, total[:, span])
 
-    if final:
-
-        @pl.when(step == NB // GROUP - 1)
-        def _():
-            for place in range(PATCH_DEV):
-                low = place * SIDE + SIDE // 2
-                image = total[:, low : low + SIDE]
+    @pl.when(step == NB // GROUP - 1)
+    def _():
+        ready = out_ref.shape[1]
+        for place in range(PATCH_DEV):
+            low = place * SIDE + SIDE // 2
+            image = total[:ready, low : low + SIDE]
+            if final:
+                out_ref[place] = image.astype(jnp.bfloat16)
+            else:
                 out_ref[place, :16] = (image[:16] + weight_ref[place]).astype(jnp.bfloat16)
                 out_ref[place, 16:] = image[16:].astype(jnp.bfloat16)
+        if not final:
+            after_ref[...] = total[ready:, :]
+
+
+def place_kernel(placing_ref, tiles_ref, terms_ref, out_ref):
+    out_ref[...] = jnp.dot(
+        placing_ref[...], tiles_ref[...], preferred_element_type=jnp.float32
+    ).astype(jnp.bfloat16)
+
+    @pl.when(pl.program_id(0) == pl.num_programs(0) - 1)
+    def _():
+        last = out_ref.shape[1] - SIDE
+        out_ref[:, last:] = jnp.dot(
+            placing_ref[...], terms_ref[...], preferred_element_type=jnp.float32
+        ).astype(jnp.bfloat16)
+
+
+def place_first(placing, tiles, terms):
+    slots, tile_count = placing.shape
+    steps = 9
+    width = (FIRST + 1) * SIDE // steps
+    return pl.pallas_call(
+        place_kernel,
+        grid=(steps,),
+        out_shape=jax.ShapeDtypeStruct((slots, steps * width), jnp.bfloat16),
+        in_specs=[
+            pl.BlockSpec((slots, tile_count), lambda s: (0, 0)),
+            pl.BlockSpec((tile_count, width), lambda s: (0, s)),
+            pl.BlockSpec((tile_count, SIDE), lambda s: (0, 0)),
+        ],
+        out_specs=pl.BlockSpec((slots, width), lambda s: (0, s)),
+        compiler_params=pltpu.CompilerParams(vmem_limit_bytes=16 * 1024 * 1024),
+        cost_estimate=pl.CostEstimate(
+            flops=2 * slots * tile_count * steps * width,
+            bytes_accessed=2 * (slots + tile_count) * steps * width,
+            transcendentals=0,
+        ),
+    )(placing, tiles, terms)
 
 
 def filter_tiles(lines, mix, got, col_band, row_band, before=None, weight=None):
@@ -162,27 +198,32 @@
     count = GROUP * PATCH_DEV
     blocks = PATCH_DEV + 1
     final = before is not None
+    rows = row_band.shape[1]
     args = [mix, got, col_band, row_band]
     in_specs = [
         pl.BlockSpec((count, slots), lambda s: (s, 0)),
         pl.BlockSpec((slots, pixels), lambda s: (0, 0)),
         pl.BlockSpec((GROUP, 2 * SIDE, SIDE), lambda s: (s, 0, 0)),
-        pl.BlockSpec((1, OUT_ROWS, GROUP * lines), lambda s: (s, 0, 0)),
+        pl.BlockSpec((1, rows, GROUP * lines), lambda s: (s, 0, 0)),
     ]
-    whole = pl.BlockSpec((OUT_ROWS, blocks * SIDE), lambda s: (0, 0))
+    later = pl.BlockSpec((OUT_ROWS - FIRST, blocks * SIDE), lambda s: (0, 0))
     scratch = [
         pltpu.VMEM((lines * count, SIDE), jnp.float32),
         pltpu.VMEM((blocks * lines, 2 * SIDE), jnp.bfloat16),
         pltpu.VMEM((GROUP * lines, blocks * SIDE), jnp.bfloat16),
+        pltpu.VMEM((rows, blocks * SIDE), jnp.float32),
     ]
-    out_shape = jax.ShapeDtypeStruct((OUT_ROWS, blocks * SIDE), jnp.float32)
-    out_specs = whole
+    ready = rows if final else FIRST
+    out_shape = [jax.ShapeDtypeStruct((PATCH_DEV, ready, SIDE), jnp.bfloat16)]
+    out_specs = [pl.BlockSpec((PATCH_DEV, ready, SIDE), lambda s: (0, 0, 0))]
     if final:
-        args += [before, weight]
-        in_specs += [whole, pl.BlockSpec((PATCH_DEV, 16, SIDE), lambda s: (0, 0, 0))]
-        scratch += [pltpu.VMEM((OUT_ROWS, blocks * SIDE), jnp.float32)]
-        out_shape = jax.ShapeDtypeStruct((PATCH_DEV, OUT_ROWS, SIDE), jnp.bfloat16)
-        out_specs = pl.BlockSpec((PATCH_DEV, OUT_ROWS, SIDE), lambda s: (0, 0, 0))
+        args += [before]
+        in_specs += [later]
+    else:
+        args += [weight]
+        in_specs += [pl.BlockSpec((PATCH_DEV, 16, SIDE), lambda s: (0, 0, 0))]
+        out_shape += [jax.ShapeDtypeStruct((OUT_ROWS - FIRST, blocks * SIDE), jnp.float32)]
+        out_specs += [later]
     return pl.pallas_call(
         functools.partial(filter_kernel, final, lines),
         grid=(steps,),
@@ -223,7 +264,7 @@
         )
 
     cut = FIRST * SIDE
-    got_first = exchange(place(jnp.concatenate([tiles[:, :cut], terms], axis=1)))
+    got_first = exchange(place_first(placing, tiles, terms))
     got_first, held = lax.optimization_barrier((got_first, place(tiles[:, cut:])))
     got_second = exchange(held)
     got_terms = got_first[:, cut:]
@@ -244,16 +285,20 @@
     row_band = tap_band(row_taps, narrow[None, :] - out_index[:, None] + TOP + HALF)
     row_band = row_band.reshape(NB // GROUP, GROUP, OUT_ROWS, SIDE).transpose(0, 2, 1, 3)
     row_first = row_band[..., :FIRST].reshape(NB // GROUP, OUT_ROWS, -1)
-    row_second = row_band[..., FIRST:].reshape(NB // GROUP, OUT_ROWS, -1)
-    partial = filter_tiles(FIRST, mix, got_first, col_band, row_first)
-    stacked = filter_tiles(
-        SIDE - FIRST, mix, got_second, col_band, row_second, partial, weight_rows
-    )
-
-    parts = lax.all_to_all(stacked, "z", split_axis=0, concat_axis=0, tiled=True)
-    parts = parts.reshape(depth, share, OUT_ROWS, SIDE).astype(jnp.float32)
+    row_second = row_band[:, FIRST:, :, FIRST:].reshape(NB // GROUP, OUT_ROWS - FIRST, -1)
+    early, partial = filter_tiles(
+        FIRST, mix, got_first, col_band, row_first, weight=weight_rows
+    )
+    (late,) = filter_tiles(SIDE - FIRST, mix, got_second, col_band, row_second, before=partial)
+
+    def to_shares(values):
+        parts = lax.all_to_all(values, "z", split_axis=0, concat_axis=0, tiled=True)
+        return parts.reshape(depth, share, -1, SIDE).astype(jnp.float32)
+
+    parts = to_shares(early)
+    plane_weight = jnp.sum(parts[:, :, :2], axis=(0, 2))
     summed = jnp.sum(parts, axis=0).astype(jnp.bfloat16)
-    plane_weight = jnp.sum(parts[:, :, :2], axis=(0, 2))
+    summed_late = jnp.sum(to_shares(late), axis=0).astype(jnp.bfloat16)
 
     def to_owner(values, shift):
         pairs = []
@@ -265,9 +310,12 @@
                         pairs.append(((v * depth + q) * cores + c, q * owners + target))
         return lax.ppermute(values, every, pairs).astype(jnp.float32)
 
-    center = to_owner(summed[:, TOP : TOP + SIDE], 0)
+    head = to_owner(summed[:, TOP:], 0)
+    tail = to_owner(summed_late[:, : TOP + SIDE - FIRST], 0)
+    center = jnp.concatenate([head, tail], axis=1)
     lower = to_owner(summed[:, TOP - HALF : TOP], -1)
-    upper = to_owner(summed[:, TOP + SIDE : TOP + SIDE + HALF], 1)
+    low = TOP + SIDE - FIRST
+    upper = to_owner(summed_late[:, low : low + HALF], 1)
     own_weight = to_owner(plane_weight, 0)
     rest = ((0, 0), (0, SIDE - HALF), (0, 0))
     numerator = center + jnp.pad(upper, rest)

time: 180 us -> 166 us (0.922); the launches traced: 177 us -> 165 us
  blocking collectives: 31.3 us -> 0 us
  starting transfers between devices: 21.8 us -> 36.7 us
  waiting for transfers between devices: 41.3 us -> 45.8 us
  other arithmetic: 4.2 us -> 8.3 us
  matrix products: 9.1 us -> 6.02 us
  local copies, waits for them, and re-layouts: 16.8 us -> 14.1 us
    all_to_all x1 -> x0, blocking collectives: 31.3 us -> none  [plane_body(): lax.all_to_all(stacked, 'z', split_axis=0, concat_axis=0, tiled=True)]
    all_to_all x0 -> x2, starting transfers between devices: none -> 9.84 us  [to_shares(): parts = lax.all_to_all(values, 'z', split_axis=0, concat_axis=0, tiled=True)]
    all_to_all x0 -> x2, waiting for transfers between devices: none -> 6.91 us  [to_shares(): parts = lax.all_to_all(values, 'z', split_axis=0, concat_axis=0, tiled=True)]
    ppermute x4 -> x5, starting transfers between devices: 12.1 us -> 17.1 us  [to_owner(): return lax.ppermute(values, every, pairs).astype(jnp.float32)]
    unnamed x15 -> x12, local copies, waits for them, and re-layouts: 0.68 us -> 4.69 us
    slice x5 -> x6, local copies, waits for them, and re-layouts: 4.54 us -> 0.55 us  [the longest x2 0.51 us: plane_body(): row_band[:, FIRST:, :, FIRST:].reshape(NB // GROUP, OUT_ROWS - FIRST, -1)]
    ppermute x4 -> x5, waiting for transfers between devices: 9.71 us -> 6.21 us  [to_owner(): return lax.ppermute(values, every, pairs).astype(jnp.float32)]
    pallas_call x0 -> x1, Pallas kernels: none -> 3.39 us  [place_first(): pl.pallas_call(place_kernel, grid=(steps,), out_shape=jax.ShapeDtypeStruc...]
  transfers between devices with their start and end apart: 6 -> 9, of which waited for: 2 -> 3; matrix products, arithmetic and copies ran while one was open for 9% -> 9% of each run, Pallas kernels for 17% -> 31%
where the time goes in v3:
time: 166 us; the launch traced here: 165 us
  Pallas kernels  54.3 us (33%)
  waiting for transfers between devices  45.8 us (28%)
  starting transfers between devices  36.7 us (22%)
  local copies, waits for them, and re-layouts  14.1 us (8%)
  other arithmetic  8.3 us (5%)
  matrix products  6.02 us (4%)
    pallas_call x2, Pallas kernels, filter_tiles(): pl.pallas_call(functools.partial(filter_kernel, final, lines), grid=(step...  50.9 us
    all_to_all x2, waiting for transfers between devices, exchange(): lax.all_to_all(values, ('visit', 'core'), split_axis=0, concat_axis=0, ti...  32.7 us
    ppermute x5, starting transfers between devices, to_owner(): return lax.ppermute(values, every, pairs).astype(jnp.float32)  17.1 us
    all_to_all x2, starting transfers between devices, to_shares(): parts = lax.all_to_all(values, 'z', split_axis=0, concat_axis=0, tiled=True)  9.84 us
    all_to_all x2, starting transfers between devices, exchange(): lax.all_to_all(values, ('visit', 'core'), split_axis=0, concat_axis=0, ti...  9.72 us
    all_to_all x2, waiting for transfers between devices, to_shares(): parts = lax.all_to_all(values, 'z', split_axis=0, concat_axis=0, tiled=True)  6.91 us
    ppermute x5, waiting for transfers between devices, to_owner(): return lax.ppermute(values, every, pairs).astype(jnp.float32)  6.21 us
    unnamed x12, local copies, waits for them, and re-layouts  4.69 us
  transfers between devices with their start and end apart: 9, of which 3 were waited for; matrix products, arithmetic and copies ran while one was open for 9% of the time, Pallas kernels for 31%

profile of v3, /device:TPU:3, one launch (start us, length us, event | category | flops | bytes accessed | tf_op | source)
XLA Modules:
  0.0 165.5 jit_solution(10270030222033818493)
XLA Ops:
  0.0 0.0 copy-start
  0.0 0.7 fusion.10
  0.8 0.1 reduce_window_sum.11
  0.9 0.8 select_reduce_fusion
  1.7 0.7 add_add_fusion
  2.4 0.7 convert_bitcast_fusion
  3.1 0.1 copy.28
  3.2 0.7 fusion.11
  4.0 0.8 copy.27
  4.8 0.7 multiply_convert_fusion
  5.5 0.1 pad.30.clone
  5.6 0.1 maximum_maximum_fusion.terms_ref
  5.7 0.0 copy-start.2
  5.7 1.9 %copy-done.2 = bf16[96,16384]{1,0:T(8,128)(2,1)S(1)} copy-done((bf16[96,16384]{1,0:T(8,128)(2,1)S(1)}, bf16[96,16384]{1,0:T(8,128)(2,1)}, u32[]{:S(2)}) %copy-start.2) | copy-done | bytes 3145752
  7.6 3.4 %shard_map.73 = bf16[192,10368]{1,0:T(8,128)(2,1)S(1)} custom-call(bf16[192,96]{1,0:T(8,128)(2,1)S(1)} %fusion.8.placing_ref, bf16[96,16384]{1,0:T(8,128)(2,1)S(1)} %copy-done.2, bf16[96,128]{1,0:T(8,128)(2,1)S(1)} %maximum_maximum_fusion.terms_ref), custom_call_target="tpu_custom_call" | custom-call | flops 382205952 | bytes 5971968 | tf_op jit(solution)/shard_map/pallas_call | solution.py:176
  11.0 0.0 copy-start.1
  11.0 1.9 %copy-done.1 = bf16[192,10368]{1,0:T(8,128)(2,1)} copy-done((bf16[192,10368]{1,0:T(8,128)(2,1)}, bf16[192,10368]{1,0:T(8,128)(2,1)S(1)}, u32[]{:S(2)}) %copy-start.1) | copy-done | bytes 3981336
  12.9 4.6 %all-to-all-start = ((bf16[8,24,10368]{2,1,0:T(8,128)(2,1)}), bf16[8,24,10368]{2,1,0:T(8,128)(2,1)}, u32[]{:S(2)}, u32[]{:S(2)}) async-start(bf16[8,24,10368]{2,1,0:T(8,128)(2,1)} %bitcast.39), calls=%async_computation | async-start | bytes 7962624 | tf_op jit(solution)/shard_map/all_to_all | solution.py:262
  17.5 0.0 copy-done
  17.5 1.5 fusion
  19.0 0.0 copy-start.4
  19.0 1.9 %copy.43 = bf16[256,128,27]{1,0,2:T(8,128)(2,1)} copy(bf16[256,128,27]{1,2,0:T(8,128)(2,1)S(1)} %fusion) | data formatting | bytes 3538944 | tf_op jit(solution)/shard_map/qrj,bj->bqr/dot_general | solution.py:38
  20.9 0.0 copy-done.4
  20.9 1.0 fusion.6
  22.0 0.5 copy.32
  22.4 0.2 slice.56
  22.7 0.3 copy.36
  23.0 0.9 copy.37.row_ref
  23.9 1.2 copy.33
  25.1 1.5 copy.35.row_ref
  26.5 3.5 %convolution_convert_fusion = bf16[192,6144]{1,0:T(8,128)(2,1)} fusion(bf16[96,16384]{1,0:T(8,128)(2,1)} %tiles_ref.1, s32[96]{0:T(128)S(1)} %add_add_fusion), kind=kOutput, calls=%fused_computation | convolution fusion | flops 227690496 | bytes 3539328 | tf_op jit(solution)/shard_map/dot_general | solution.py:259
  30.0 32.7 %all-to-all-done = bf16[8,24,10368]{2,1,0:T(8,128)(2,1)} async-done(((bf16[8,24,10368]{2,1,0:T(8,128)(2,1)}), bf16[8,24,10368]{2,1,0:T(8,128)(2,1)}, u32[]{:S(2)}, u32[]{:S(2)}) %all-to-all-start) | async-done | bytes 3981344 | tf_op jit(solution)/shard_map/all_to_all | solution.py:262
  62.8 0.9 slice_bitcast_fusion.1
  63.6 0.8 slice_bitcast_fusion
  64.4 1.0 convert_reduce_fusion
  65.4 0.1 copy.30
  65.5 0.1 copy.29
  65.6 5.2 %all-to-all-start.2 = ((bf16[8,24,6144]{2,1,0:T(8,128)(2,1)}), bf16[8,24,6144]{2,1,0:T(8,128)(2,1)S(1)}, u32[]{:S(2)}, u32[]{:S(2)}) async-start(bf16[8,24,6144]{2,1,0:T(8,128)(2,1)} %bitcast.16), calls=%async_computation.2 | async-start | bytes 4718592 | tf_op jit(solution)/shard_map/all_to_all | solution.py:262
  70.8 0.9 multiply_reduce_fusion
  71.7 0.1 copy.39
  71.8 0.8 broadcast_multiply_fusion
  72.6 0.8 broadcast_in_dim.10.rest_0_
  73.4 30.9 %shard_map.74 = (bf16[24,80,128]{2,1,0:T(8,128)(2,1)}, f32[96,3200]{1,0:T(8,128)}) custom-call(bf16[648,192]{1,0:T(8,128)(2,1)} %bitcast.50, bf16[192,10368]{1,0:T(8,128)(2,1)} %bitcast.3.got_ref, bf16[27,256,128]{2,1,0:T(8,128)(2,1)} %bitcast.47, bf16[3,176,720]{2,1,0:T(8,128)(2,1)} %copy.35.row_ref, f32[24,16,128]{2,1,0:T(8,128)} %broadcast_in_dim.10.rest_0_), custom_call_target="tpu_custom_call" | custom-call | flops 16000000000 | bytes 8000000 | tf_op jit(solution)/shard_map/pallas_call | solution.py:227
  104.2 0.0 all-to-all-done.2
  104.2 0.0 copy-start.3
  104.2 5.3 %all-to-all-start.1 = ((bf16[24,80,128]{2,1,0:T(8,128)(2,1)}), bf16[24,80,128]{2,1,0:T(8,128)(2,1)S(1)}, u32[]{:S(2)}, u32[]{:S(2)}) async-start(bf16[24,80,128]{2,1,0:T(8,128)(2,1)} %get-tuple-element.10), calls=%async_computation.1 | async-start | bytes 983040 | tf_op jit(solution)/shard_map/all_to_all | solution.py:295
  109.5 0.0 copy-done.3
  109.5 20.0 %shard_map.75 = bf16[24,96,128]{2,1,0:T(8,128)(2,1)} custom-call(bf16[648,192]{1,0:T(8,128)(2,1)} %bitcast.51, bf16[192,6144]{1,0:T(8,128)(2,1)} %bitcast.43, bf16[27,256,128]{2,1,0:T(8,128)(2,1)} %bitcast.48, bf16[3,96,432]{2,1,0:T(8,128)(2,1)} %copy.37.row_ref, f32[96,3200]{1,0:T(8,128)} %get-tuple-element.12.rest_0_), custom_call_target="tpu_custom_call" | custom-call | flops 9600000000 | bytes 4800000 | tf_op jit(solution)/shard_map/pallas_call | solution.py:227
  129.6 0.0 all-to-all-done.1
  129.6 4.5 %all-to-all-start.3 = ((bf16[24,96,128]{2,1,0:T(8,128)(2,1)}), bf16[24,96,128]{2,1,0:T(8,128)(2,1)S(1)}, u32[]{:S(2)}, u32[]{:S(2)}) async-start(bf16[24,96,128]{2,1,0:T(8,128)(2,1)} %shard_map.75), calls=%async_computation.3 | async-start | bytes 1179648 | tf_op jit(solution)/shard_map/all_to_all | solution.py:295
  134.1 3.2 %collective-permute-start.4 = (f32[6,128]{1,0:T(8,128)S(1)}, f32[6,128]{1,0:T(8,128)S(1)}, u32[]{:S(2)}, u32[]{:S(2)}) collective-permute-start(f32[6,128]{1,0:T(8,128)S(1)} %convert_reduce_fusion.1), channel_id=1, source_target_pairs={{0,0},{1,1},{2,8},{3,9},{4,16},{5,17},{6,24},{7,25},{8,2},{9,3},{1... | collective-permute-start | bytes 9224 | tf_op jit(solution)/shard_map/ppermute | solution.py:311
  137.4 0.1 reduce_sum.56
  137.5 3.0 %collective-permute-start = (bf16[6,56,128]{2,1,0:T(8,128)(2,1)S(1)}, bf16[6,56,128]{2,1,0:T(8,128)(2,1)S(1)}, u32[]{:S(2)}, u32[]{:S(2)}) collective-permute-start(bf16[6,56,128]{2,1,0:T(8,128)(2,1)S(1)} %slice.55), channel_id=1, source_target_pairs={{0,0},{1,1},{2,8},{3,9},{4,16},{5,17},{6,24},{7,25},{8,2},{9,3},{1... | collective-permute-start | bytes 258056 | tf_op jit(solution)/shard_map/ppermute | solution.py:311
  140.5 4.9 %collective-permute-start.3 = (bf16[6,20,128]{2,1,0:T(8,128)(2,1)S(1)}, bf16[6,20,128]{2,1,0:T(8,128)(2,1)S(1)}, u32[]{:S(2)}, u32[]{:S(2)}) collective-permute-start(bf16[6,20,128]{2,1,0:T(8,128)(2,1)S(1)} %slice.59), channel_id=1, source_target_pairs={{1,0},{3,8},{5,16},{7,24},{8,1},{9,2},{10,9},{11,10},{12,17},{13,1... | collective-permute-start | bytes 92168 | tf_op jit(solution)/shard_map/ppermute | solution.py:311
  145.3 6.9 %all-to-all-done.3 = bf16[24,96,128]{2,1,0:T(8,128)(2,1)S(1)} async-done(((bf16[24,96,128]{2,1,0:T(8,128)(2,1)}), bf16[24,96,128]{2,1,0:T(8,128)(2,1)S(1)}, u32[]{:S(2)}, u32[]{:S(2)}) %all-to-all-start.3) | async-done | bytes 589856 | tf_op jit(solution)/shard_map/all_to_all | solution.py:295
  152.2 0.1 reduce_sum.57
  152.4 1.9 %collective-permute-start.1 = (bf16[6,72,128]{2,1,0:T(8,128)(2,1)S(1)}, bf16[6,72,128]{2,1,0:T(8,128)(2,1)S(1)}, u32[]{:S(2)}, u32[]{:S(2)}) collective-permute-start(bf16[6,72,128]{2,1,0:T(8,128)(2,1)S(1)} %slice.57), channel_id=1, source_target_pairs={{0,0},{1,1},{2,8},{3,9},{4,16},{5,17},{6,24},{7,25},{8,2},{9,3},{1... | collective-permute-start | bytes 331784 | tf_op jit(solution)/shard_map/ppermute | solution.py:311
  154.3 4.1 %collective-permute-start.2 = (bf16[6,20,128]{2,1,0:T(8,128)(2,1)S(1)}, bf16[6,20,128]{2,1,0:T(8,128)(2,1)S(1)}, u32[]{:S(2)}, u32[]{:S(2)}) collective-permute-start(bf16[6,20,128]{2,1,0:T(8,128)(2,1)S(1)} %slice.58), channel_id=1, source_target_pairs={{0,1},{1,2},{2,9},{3,10},{4,17},{5,18},{6,25},{7,26},{8,3},{9,4},{... | collective-permute-start | bytes 92168 | tf_op jit(solution)/shard_map/ppermute | solution.py:311
  158.4 0.0 collective-permute-done.4
  158.4 0.0 collective-permute-done.3
  158.5 0.0 collective-permute-done
  158.5 6.2 %collective-permute-done.2 = bf16[6,20,128]{2,1,0:T(8,128)(2,1)S(1)} collective-permute-done((bf16[6,20,128]{2,1,0:T(8,128)(2,1)S(1)}, bf16[6,20,128]{2,1,0:T(8,128)(2,1)S(1)}, u32[]{:S(2)}, u32[]{:S(2)}) %collective-permute-start.2) | collective-permute-done | bytes 30752 | tf_op jit(solution)/shard_map/ppermute | solution.py:311
  164.7 0.0 collective-permute-done.1
  164.7 0.8 divide_bitcast_fusion
  (13 shorter events, 0.1 us)
Async XLA Ops:
  0.0 17.5 %copy-start = (bf16[27,41]{1,0:T(8,128)(2,1)S(1)}, bf16[27,41]{1,0:T(8,128)(2,1)}, u32[]{:S(2)}) copy-start(bf16[27,41]{1,0:T(8,128)(2,1)} %param.13) | copy-start | bytes 6646
  5.7 1.9 %copy-start.2 = (bf16[96,16384]{1,0:T(8,128)(2,1)S(1)}, bf16[96,16384]{1,0:T(8,128)(2,1)}, u32[]{:S(2)}) copy-start(bf16[96,16384]{1,0:T(8,128)(2,1)} %tiles_ref.1) | copy-start | bytes 9437188
  11.0 1.9 %copy-start.1 = (bf16[192,10368]{1,0:T(8,128)(2,1)}, bf16[192,10368]{1,0:T(8,128)(2,1)S(1)}, u32[]{:S(2)}) copy-start(bf16[192,10368]{1,0:T(8,128)(2,1)S(1)} %shard_map.73) | copy-start | bytes 11943940
  12.9 49.9 %all-to-all-start = ((bf16[8,24,10368]{2,1,0:T(8,128)(2,1)}), bf16[8,24,10368]{2,1,0:T(8,128)(2,1)}, u32[]{:S(2)}, u32[]{:S(2)}) async-start(bf16[8,24,10368]{2,1,0:T(8,128)(2,1)} %bitcast.39), calls=%async_computation | async-start | bytes 7962624 | tf_op jit(solution)/shard_map/all_to_all | solution.py:262
  19.0 1.9 %copy-start.4 = (bf16[27,41]{1,0:T(8,128)(2,1)S(1)}, bf16[27,41]{1,0:T(8,128)(2,1)}, u32[]{:S(2)}) copy-start(bf16[27,41]{1,0:T(8,128)(2,1)} %param.12) | copy-start | bytes 6646
  65.6 38.6 %all-to-all-start.2 = ((bf16[8,24,6144]{2,1,0:T(8,128)(2,1)}), bf16[8,24,6144]{2,1,0:T(8,128)(2,1)S(1)}, u32[]{:S(2)}, u32[]{:S(2)}) async-start(bf16[8,24,6144]{2,1,0:T(8,128)(2,1)} %bitcast.16), calls=%async_computation.2 | async-start | bytes 4718592 | tf_op jit(solution)/shard_map/all_to_all | solution.py:262
  104.2 5.3 %copy-start.3 = (bf16[8,24,6144]{2,1,0:T(8,128)(2,1)}, bf16[8,24,6144]{2,1,0:T(8,128)(2,1)S(1)}, u32[]{:S(2)}) copy-start(bf16[8,24,6144]{2,1,0:T(8,128)(2,1)S(1)} %all-to-all-done.2) | copy-start | bytes 7077892
  104.2 25.4 %all-to-all-start.1 = ((bf16[24,80,128]{2,1,0:T(8,128)(2,1)}), bf16[24,80,128]{2,1,0:T(8,128)(2,1)S(1)}, u32[]{:S(2)}, u32[]{:S(2)}) async-start(bf16[24,80,128]{2,1,0:T(8,128)(2,1)} %get-tuple-element.10), calls=%async_computation.1 | async-start | bytes 983040 | tf_op jit(solution)/shard_map/all_to_all | solution.py:295
  129.6 22.6 %all-to-all-start.3 = ((bf16[24,96,128]{2,1,0:T(8,128)(2,1)}), bf16[24,96,128]{2,1,0:T(8,128)(2,1)S(1)}, u32[]{:S(2)}, u32[]{:S(2)}) async-start(bf16[24,96,128]{2,1,0:T(8,128)(2,1)} %shard_map.75), calls=%async_computation.3 | async-start | bytes 1179648 | tf_op jit(solution)/shard_map/all_to_all | solution.py:295
  134.1 24.3 %collective-permute-start.4 = (f32[6,128]{1,0:T(8,128)S(1)}, f32[6,128]{1,0:T(8,128)S(1)}, u32[]{:S(2)}, u32[]{:S(2)}) collective-permute-start(f32[6,128]{1,0:T(8,128)S(1)} %convert_reduce_fusion.1), channel_id=1, source_target_pairs={{0,0},{1,1},{2,8},{3,9},{4,16},{5,17},{6,24},{7,25},{8,2},{9,3},{1... | collective-permute-start | bytes 9224 | tf_op jit(solution)/shard_map/ppermute | solution.py:311
  137.5 21.0 %collective-permute-start = (bf16[6,56,128]{2,1,0:T(8,128)(2,1)S(1)}, bf16[6,56,128]{2,1,0:T(8,128)(2,1)S(1)}, u32[]{:S(2)}, u32[]{:S(2)}) collective-permute-start(bf16[6,56,128]{2,1,0:T(8,128)(2,1)S(1)} %slice.55), channel_id=1, source_target_pairs={{0,0},{1,1},{2,8},{3,9},{4,16},{5,17},{6,24},{7,25},{8,2},{9,3},{1... | collective-permute-start | bytes 258056 | tf_op jit(solution)/shard_map/ppermute | solution.py:311
  140.5 18.0 %collective-permute-start.3 = (bf16[6,20,128]{2,1,0:T(8,128)(2,1)S(1)}, bf16[6,20,128]{2,1,0:T(8,128)(2,1)S(1)}, u32[]{:S(2)}, u32[]{:S(2)}) collective-permute-start(bf16[6,20,128]{2,1,0:T(8,128)(2,1)S(1)} %slice.59), channel_id=1, source_target_pairs={{1,0},{3,8},{5,16},{7,24},{8,1},{9,2},{10,9},{11,10},{12,17},{13,1... | collective-permute-start | bytes 92168 | tf_op jit(solution)/shard_map/ppermute | solution.py:311
  152.4 12.3 %collective-permute-start.1 = (bf16[6,72,128]{2,1,0:T(8,128)(2,1)S(1)}, bf16[6,72,128]{2,1,0:T(8,128)(2,1)S(1)}, u32[]{:S(2)}, u32[]{:S(2)}) collective-permute-start(bf16[6,72,128]{2,1,0:T(8,128)(2,1)S(1)} %slice.57), channel_id=1, source_target_pairs={{0,0},{1,1},{2,8},{3,9},{4,16},{5,17},{6,24},{7,25},{8,2},{9,3},{1... | collective-permute-start | bytes 331784 | tf_op jit(solution)/shard_map/ppermute | solution.py:311
  154.3 10.4 %collective-permute-start.2 = (bf16[6,20,128]{2,1,0:T(8,128)(2,1)S(1)}, bf16[6,20,128]{2,1,0:T(8,128)(2,1)S(1)}, u32[]{:S(2)}, u32[]{:S(2)}) collective-permute-start(bf16[6,20,128]{2,1,0:T(8,128)(2,1)S(1)} %slice.58), channel_id=1, source_target_pairs={{0,1},{1,2},{2,9},{3,10},{4,17},{5,18},{6,25},{7,26},{8,3},{9,4},{... | collective-permute-start | bytes 92168 | tf_op jit(solution)/shard_map/ppermute | solution.py:311

commit v4 on v3

--- a/solution.py
+++ b/solution.py
@@ -106,9 +106,9 @@
         both = jnp.dot(
             mix_ref[...], got_ref[:, pl.ds(start, 2 * SIDE)], preferred_element_type=jnp.float32
         )
-        row = pl.multiple_of(pair * 2 * count, 8)
+        row = pair * 2 * (count + 1)
         planes[pl.ds(row, count), :] = both[:, :SIDE]
-        planes[pl.ds(pl.multiple_of(row + count, 8), count), :] = both[:, SIDE:]
+        planes[pl.ds(row + count + 1, count), :] = both[:, SIDE:]
         return carry
 
     lax.fori_loop(0, lines // 2, make_planes, 0, unroll=4)
@@ -120,7 +120,7 @@
 
     def filter_columns(basis, carry):
         for place in range(PATCH_DEV):
-            image = planes[pl.ds(basis * PATCH_DEV + place, lines, stride=count), :]
+            image = planes[pl.ds(basis * PATCH_DEV + place, lines, stride=count + 1), :]
             image = image.astype(jnp.bfloat16)
             strip[place * lines : (place + 1) * lines, SIDE:] = image
             strip[(place + 1) * lines : (place + 2) * lines, :SIDE] = image
@@ -183,7 +183,7 @@
             pl.BlockSpec((tile_count, SIDE), lambda s: (0, 0)),
         ],
         out_specs=pl.BlockSpec((slots, width), lambda s: (0, s)),
-        compiler_params=pltpu.CompilerParams(vmem_limit_bytes=16 * 1024 * 1024),
+        compiler_params=pltpu.CompilerParams(vmem_limit_bytes=56 * 1024 * 1024),
         cost_estimate=pl.CostEstimate(
             flops=2 * slots * tile_count * steps * width,
             bytes_accessed=2 * (slots + tile_count) * steps * width,
@@ -208,7 +208,7 @@
     ]
     later = pl.BlockSpec((OUT_ROWS - FIRST, blocks * SIDE), lambda s: (0, 0))
     scratch = [
-        pltpu.VMEM((lines * count, SIDE), jnp.float32),
+        pltpu.VMEM((lines * (count + 1) + 16, SIDE), jnp.float32),
         pltpu.VMEM((blocks * lines, 2 * SIDE), jnp.bfloat16),
         pltpu.VMEM((GROUP * lines, blocks * SIDE), jnp.bfloat16),
         pltpu.VMEM((rows, blocks * SIDE), jnp.float32),

time: 166 us -> 167 us (level)
  local copies, waits for them, and re-layouts: 14.1 us -> 10.3 us
  Pallas kernels: 54.3 us -> 57.2 us
    pallas_call x1, Pallas kernels: 3.39 us -> 7.66 us  [place_first(): pl.pallas_call(place_kernel, grid=(steps,), out_shape=jax.ShapeDtypeStruc...]
    unnamed x12 -> x8, local copies, waits for them, and re-layouts: 4.69 us -> 0.91 us
  transfers between devices with their start and end apart: 9 -> 9, of which waited for: 3 -> 3; matrix products, arithmetic and copies ran while one was open for 9% -> 9% of each run, Pallas kernels for 31% -> 30%
where the time goes in v4:
time: 167 us; the launch traced here: 166 us
  Pallas kernels  57.2 us (34%)
  waiting for transfers between devices  45.8 us (27%)
  starting transfers between devices  36.7 us (22%)
  local copies, waits for them, and re-layouts  10.3 us (6%)
  other arithmetic  9.51 us (6%)
  matrix products  6.03 us (4%)
    pallas_call x2, Pallas kernels, filter_tiles(): pl.pallas_call(functools.partial(filter_kernel, final, lines), grid=(step...  49.5 us
    all_to_all x2, waiting for transfers between devices, exchange(): lax.all_to_all(values, ('visit', 'core'), split_axis=0, concat_axis=0, ti...  32.7 us
    ppermute x5, starting transfers between devices, to_owner(): return lax.ppermute(values, every, pairs).astype(jnp.float32)  17.1 us
    all_to_all x2, starting transfers between devices, to_shares(): parts = lax.all_to_all(values, 'z', split_axis=0, concat_axis=0, tiled=True)  9.85 us
    all_to_all x2, starting transfers between devices, exchange(): lax.all_to_all(values, ('visit', 'core'), split_axis=0, concat_axis=0, ti...  9.73 us
    pallas_call x1, Pallas kernels, place_first(): pl.pallas_call(place_kernel, grid=(steps,), out_shape=jax.ShapeDtypeStruc...  7.66 us
    all_to_all x2, waiting for transfers between devices, to_shares(): parts = lax.all_to_all(values, 'z', split_axis=0, concat_axis=0, tiled=True)  6.89 us
    ppermute x5, waiting for transfers between devices, to_owner(): return lax.ppermute(values, every, pairs).astype(jnp.float32)  6.22 us
  transfers between devices with their start and end apart: 9, of which 3 were waited for; matrix products, arithmetic and copies ran while one was open for 9% of the time, Pallas kernels for 30%

profile of v4, /device:TPU:3, one launch (start us, length us, event | category | flops | bytes accessed | tf_op | source)
XLA Modules:
  0.0 165.8 jit_solution(190873111671838484)
XLA Ops:
  0.0 0.0 copy-start
  0.0 0.7 fusion.10
  0.8 0.1 reduce_window_sum.11
  0.9 0.8 select_reduce_fusion
  1.7 0.7 add_add_fusion
  2.4 0.6 fusion.8.placing_ref
  3.0 0.7 convert_bitcast_fusion
  3.7 0.1 copy.28
  3.8 0.7 fusion.11
  4.6 0.8 copy.27
  5.4 0.7 multiply_convert_fusion
  6.1 0.1 pad.30.clone
  6.2 0.7 maximum_maximum_fusion.terms_ref
  6.9 7.7 %shard_map.73 = bf16[192,10368]{1,0:T(8,128)(2,1)} custom-call(bf16[192,96]{1,0:T(8,128)(2,1)} %fusion.8.placing_ref, bf16[96,16384]{1,0:T(8,128)(2,1)} %tiles_ref.1, bf16[96,128]{1,0:T(8,128)(2,1)} %maximum_maximum_fusion.terms_ref), custom_call_target="tpu_custom_call" | custom-call | flops 382205952 | bytes 5971968 | tf_op jit(solution)/shard_map/pallas_call | solution.py:176
  14.5 4.6 %all-to-all-start = ((bf16[8,24,10368]{2,1,0:T(8,128)(2,1)}), bf16[8,24,10368]{2,1,0:T(8,128)(2,1)}, u32[]{:S(2)}, u32[]{:S(2)}) async-start(bf16[8,24,10368]{2,1,0:T(8,128)(2,1)} %bitcast.39), calls=%async_computation | async-start | bytes 7962624 | tf_op jit(solution)/shard_map/all_to_all | solution.py:262
  19.1 0.0 copy-done
  19.1 1.5 fusion
  20.6 0.0 copy-start.2
  20.7 1.9 %copy.43 = bf16[256,128,27]{1,0,2:T(8,128)(2,1)} copy(bf16[256,128,27]{1,2,0:T(8,128)(2,1)S(1)} %fusion) | data formatting | bytes 3538944 | tf_op jit(solution)/shard_map/qrj,bj->bqr/dot_general | solution.py:38
  22.6 0.0 copy-done.2
  22.6 1.0 fusion.6
  23.6 0.5 copy.32
  24.1 0.2 slice.56
  24.4 0.3 copy.36
  24.7 0.9 copy.37.row_ref
  25.6 1.2 copy.33
  26.8 1.5 copy.35.row_ref
  28.2 3.5 %convolution_convert_fusion = bf16[192,6144]{1,0:T(8,128)(2,1)} fusion(bf16[96,16384]{1,0:T(8,128)(2,1)} %tiles_ref.1, s32[96]{0:T(128)S(1)} %add_add_fusion), kind=kOutput, calls=%fused_computation | convolution fusion | flops 227690496 | bytes 3539328 | tf_op jit(solution)/shard_map/dot_general | solution.py:259
  31.7 32.7 %all-to-all-done = bf16[8,24,10368]{2,1,0:T(8,128)(2,1)} async-done(((bf16[8,24,10368]{2,1,0:T(8,128)(2,1)}), bf16[8,24,10368]{2,1,0:T(8,128)(2,1)}, u32[]{:S(2)}, u32[]{:S(2)}) %all-to-all-start) | async-done | bytes 3981344 | tf_op jit(solution)/shard_map/all_to_all | solution.py:262
  64.4 0.9 slice_bitcast_fusion.1
  65.3 0.8 slice_bitcast_fusion
  66.1 1.0 convert_reduce_fusion
  67.1 0.1 copy.30
  67.2 0.1 copy.29
  67.3 5.2 %all-to-all-start.2 = ((bf16[8,24,6144]{2,1,0:T(8,128)(2,1)}), bf16[8,24,6144]{2,1,0:T(8,128)(2,1)S(1)}, u32[]{:S(2)}, u32[]{:S(2)}) async-start(bf16[8,24,6144]{2,1,0:T(8,128)(2,1)} %bitcast.16), calls=%async_computation.2 | async-start | bytes 4718592 | tf_op jit(solution)/shard_map/all_to_all | solution.py:262
  72.4 0.9 multiply_reduce_fusion
  73.4 0.1 copy.39
  73.5 0.8 broadcast_multiply_fusion
  74.2 0.8 broadcast_in_dim.10.rest_0_
  75.0 29.8 %shard_map.74 = (bf16[24,80,128]{2,1,0:T(8,128)(2,1)}, f32[96,3200]{1,0:T(8,128)}) custom-call(bf16[648,192]{1,0:T(8,128)(2,1)} %bitcast.50, bf16[192,10368]{1,0:T(8,128)(2,1)} %bitcast.3.got_ref, bf16[27,256,128]{2,1,0:T(8,128)(2,1)} %bitcast.47, bf16[3,176,720]{2,1,0:T(8,128)(2,1)} %copy.35.row_ref, f32[24,16,128]{2,1,0:T(8,128)} %broadcast_in_dim.10.rest_0_), custom_call_target="tpu_custom_call" | custom-call | flops 16000000000 | bytes 8000000 | tf_op jit(solution)/shard_map/pallas_call | solution.py:227
  104.9 0.0 all-to-all-done.2
  104.9 0.0 copy-start.1
  104.9 5.3 %all-to-all-start.1 = ((bf16[24,80,128]{2,1,0:T(8,128)(2,1)}), bf16[24,80,128]{2,1,0:T(8,128)(2,1)S(1)}, u32[]{:S(2)}, u32[]{:S(2)}) async-start(bf16[24,80,128]{2,1,0:T(8,128)(2,1)} %get-tuple-element.10), calls=%async_computation.1 | async-start | bytes 983040 | tf_op jit(solution)/shard_map/all_to_all | solution.py:295
  110.2 0.0 copy-done.1
  110.2 19.7 %shard_map.75 = bf16[24,96,128]{2,1,0:T(8,128)(2,1)} custom-call(bf16[648,192]{1,0:T(8,128)(2,1)} %bitcast.51, bf16[192,6144]{1,0:T(8,128)(2,1)} %bitcast.43, bf16[27,256,128]{2,1,0:T(8,128)(2,1)} %bitcast.48, bf16[3,96,432]{2,1,0:T(8,128)(2,1)} %copy.37.row_ref, f32[96,3200]{1,0:T(8,128)} %get-tuple-element.12.rest_0_), custom_call_target="tpu_custom_call" | custom-call | flops 9600000000 | bytes 4800000 | tf_op jit(solution)/shard_map/pallas_call | solution.py:227
  129.9 0.0 all-to-all-done.1
  129.9 4.5 %all-to-all-start.3 = ((bf16[24,96,128]{2,1,0:T(8,128)(2,1)}), bf16[24,96,128]{2,1,0:T(8,128)(2,1)S(1)}, u32[]{:S(2)}, u32[]{:S(2)}) async-start(bf16[24,96,128]{2,1,0:T(8,128)(2,1)} %shard_map.75), calls=%async_computation.3 | async-start | bytes 1179648 | tf_op jit(solution)/shard_map/all_to_all | solution.py:295
  134.4 3.2 %collective-permute-start.4 = (f32[6,128]{1,0:T(8,128)S(1)}, f32[6,128]{1,0:T(8,128)S(1)}, u32[]{:S(2)}, u32[]{:S(2)}) collective-permute-start(f32[6,128]{1,0:T(8,128)S(1)} %convert_reduce_fusion.1), channel_id=1, source_target_pairs={{0,0},{1,1},{2,8},{3,9},{4,16},{5,17},{6,24},{7,25},{8,2},{9,3},{1... | collective-permute-start | bytes 9224 | tf_op jit(solution)/shard_map/ppermute | solution.py:311
  137.6 0.1 reduce_sum.56
  137.7 3.0 %collective-permute-start = (bf16[6,56,128]{2,1,0:T(8,128)(2,1)S(1)}, bf16[6,56,128]{2,1,0:T(8,128)(2,1)S(1)}, u32[]{:S(2)}, u32[]{:S(2)}) collective-permute-start(bf16[6,56,128]{2,1,0:T(8,128)(2,1)S(1)} %slice.55), channel_id=1, source_target_pairs={{0,0},{1,1},{2,8},{3,9},{4,16},{5,17},{6,24},{7,25},{8,2},{9,3},{1... | collective-permute-start | bytes 258056 | tf_op jit(solution)/shard_map/ppermute | solution.py:311
  140.8 4.9 %collective-permute-start.3 = (bf16[6,20,128]{2,1,0:T(8,128)(2,1)S(1)}, bf16[6,20,128]{2,1,0:T(8,128)(2,1)S(1)}, u32[]{:S(2)}, u32[]{:S(2)}) collective-permute-start(bf16[6,20,128]{2,1,0:T(8,128)(2,1)S(1)} %slice.59), channel_id=1, source_target_pairs={{1,0},{3,8},{5,16},{7,24},{8,1},{9,2},{10,9},{11,10},{12,17},{13,1... | collective-permute-start | bytes 92168 | tf_op jit(solution)/shard_map/ppermute | solution.py:311
  145.6 6.9 %all-to-all-done.3 = bf16[24,96,128]{2,1,0:T(8,128)(2,1)S(1)} async-done(((bf16[24,96,128]{2,1,0:T(8,128)(2,1)}), bf16[24,96,128]{2,1,0:T(8,128)(2,1)S(1)}, u32[]{:S(2)}, u32[]{:S(2)}) %all-to-all-start.3) | async-done | bytes 589856 | tf_op jit(solution)/shard_map/all_to_all | solution.py:295
  152.5 0.1 reduce_sum.57
  152.7 1.9 %collective-permute-start.1 = (bf16[6,72,128]{2,1,0:T(8,128)(2,1)S(1)}, bf16[6,72,128]{2,1,0:T(8,128)(2,1)S(1)}, u32[]{:S(2)}, u32[]{:S(2)}) collective-permute-start(bf16[6,72,128]{2,1,0:T(8,128)(2,1)S(1)} %slice.57), channel_id=1, source_target_pairs={{0,0},{1,1},{2,8},{3,9},{4,16},{5,17},{6,24},{7,25},{8,2},{9,3},{1... | collective-permute-start | bytes 331784 | tf_op jit(solution)/shard_map/ppermute | solution.py:311
  154.6 4.1 %collective-permute-start.2 = (bf16[6,20,128]{2,1,0:T(8,128)(2,1)S(1)}, bf16[6,20,128]{2,1,0:T(8,128)(2,1)S(1)}, u32[]{:S(2)}, u32[]{:S(2)}) collective-permute-start(bf16[6,20,128]{2,1,0:T(8,128)(2,1)S(1)} %slice.58), channel_id=1, source_target_pairs={{0,1},{1,2},{2,9},{3,10},{4,17},{5,18},{6,25},{7,26},{8,3},{9,4},{... | collective-permute-start | bytes 92168 | tf_op jit(solution)/shard_map/ppermute | solution.py:311
  158.7 0.0 collective-permute-done.4
  158.7 0.0 collective-permute-done.3
  158.8 0.0 collective-permute-done
  158.8 6.2 %collective-permute-done.2 = bf16[6,20,128]{2,1,0:T(8,128)(2,1)S(1)} collective-permute-done((bf16[6,20,128]{2,1,0:T(8,128)(2,1)S(1)}, bf16[6,20,128]{2,1,0:T(8,128)(2,1)S(1)}, u32[]{:S(2)}, u32[]{:S(2)}) %collective-permute-start.2) | collective-permute-done | bytes 30752 | tf_op jit(solution)/shard_map/ppermute | solution.py:311
  165.0 0.0 collective-permute-done.1
  165.0 0.8 divide_bitcast_fusion
  (12 shorter events, 0.1 us)
Async XLA Ops:
  0.0 19.1 %copy-start = (bf16[27,41]{1,0:T(8,128)(2,1)S(1)}, bf16[27,41]{1,0:T(8,128)(2,1)}, u32[]{:S(2)}) copy-start(bf16[27,41]{1,0:T(8,128)(2,1)} %param.13) | copy-start | bytes 6646
  14.5 49.9 %all-to-all-start = ((bf16[8,24,10368]{2,1,0:T(8,128)(2,1)}), bf16[8,24,10368]{2,1,0:T(8,128)(2,1)}, u32[]{:S(2)}, u32[]{:S(2)}) async-start(bf16[8,24,10368]{2,1,0:T(8,128)(2,1)} %bitcast.39), calls=%async_computation | async-start | bytes 7962624 | tf_op jit(solution)/shard_map/all_to_all | solution.py:262
  20.6 1.9 %copy-start.2 = (bf16[27,41]{1,0:T(8,128)(2,1)S(1)}, bf16[27,41]{1,0:T(8,128)(2,1)}, u32[]{:S(2)}) copy-start(bf16[27,41]{1,0:T(8,128)(2,1)} %param.12) | copy-start | bytes 6646
  67.3 37.6 %all-to-all-start.2 = ((bf16[8,24,6144]{2,1,0:T(8,128)(2,1)}), bf16[8,24,6144]{2,1,0:T(8,128)(2,1)S(1)}, u32[]{:S(2)}, u32[]{:S(2)}) async-start(bf16[8,24,6144]{2,1,0:T(8,128)(2,1)} %bitcast.16), calls=%async_computation.2 | async-start | bytes 4718592 | tf_op jit(solution)/shard_map/all_to_all | solution.py:262
  104.9 5.3 %copy-start.1 = (bf16[8,24,6144]{2,1,0:T(8,128)(2,1)}, bf16[8,24,6144]{2,1,0:T(8,128)(2,1)S(1)}, u32[]{:S(2)}) copy-start(bf16[8,24,6144]{2,1,0:T(8,128)(2,1)S(1)} %all-to-all-done.2) | copy-start | bytes 7077892
  104.9 25.0 %all-to-all-start.1 = ((bf16[24,80,128]{2,1,0:T(8,128)(2,1)}), bf16[24,80,128]{2,1,0:T(8,128)(2,1)S(1)}, u32[]{:S(2)}, u32[]{:S(2)}) async-start(bf16[24,80,128]{2,1,0:T(8,128)(2,1)} %get-tuple-element.10), calls=%async_computation.1 | async-start | bytes 983040 | tf_op jit(solution)/shard_map/all_to_all | solution.py:295
  129.9 22.6 %all-to-all-start.3 = ((bf16[24,96,128]{2,1,0:T(8,128)(2,1)}), bf16[24,96,128]{2,1,0:T(8,128)(2,1)S(1)}, u32[]{:S(2)}, u32[]{:S(2)}) async-start(bf16[24,96,128]{2,1,0:T(8,128)(2,1)} %shard_map.75), calls=%async_computation.3 | async-start | bytes 1179648 | tf_op jit(solution)/shard_map/all_to_all | solution.py:295
  134.4 24.3 %collective-permute-start.4 = (f32[6,128]{1,0:T(8,128)S(1)}, f32[6,128]{1,0:T(8,128)S(1)}, u32[]{:S(2)}, u32[]{:S(2)}) collective-permute-start(f32[6,128]{1,0:T(8,128)S(1)} %convert_reduce_fusion.1), channel_id=1, source_target_pairs={{0,0},{1,1},{2,8},{3,9},{4,16},{5,17},{6,24},{7,25},{8,2},{9,3},{1... | collective-permute-start | bytes 9224 | tf_op jit(solution)/shard_map/ppermute | solution.py:311
  137.7 21.0 %collective-permute-start = (bf16[6,56,128]{2,1,0:T(8,128)(2,1)S(1)}, bf16[6,56,128]{2,1,0:T(8,128)(2,1)S(1)}, u32[]{:S(2)}, u32[]{:S(2)}) collective-permute-start(bf16[6,56,128]{2,1,0:T(8,128)(2,1)S(1)} %slice.55), channel_id=1, source_target_pairs={{0,0},{1,1},{2,8},{3,9},{4,16},{5,17},{6,24},{7,25},{8,2},{9,3},{1... | collective-permute-start | bytes 258056 | tf_op jit(solution)/shard_map/ppermute | solution.py:311
  140.8 18.0 %collective-permute-start.3 = (bf16[6,20,128]{2,1,0:T(8,128)(2,1)S(1)}, bf16[6,20,128]{2,1,0:T(8,128)(2,1)S(1)}, u32[]{:S(2)}, u32[]{:S(2)}) collective-permute-start(bf16[6,20,128]{2,1,0:T(8,128)(2,1)S(1)} %slice.59), channel_id=1, source_target_pairs={{1,0},{3,8},{5,16},{7,24},{8,1},{9,2},{10,9},{11,10},{12,17},{13,1... | collective-permute-start | bytes 92168 | tf_op jit(solution)/shard_map/ppermute | solution.py:311
  152.7 12.3 %collective-permute-start.1 = (bf16[6,72,128]{2,1,0:T(8,128)(2,1)S(1)}, bf16[6,72,128]{2,1,0:T(8,128)(2,1)S(1)}, u32[]{:S(2)}, u32[]{:S(2)}) collective-permute-start(bf16[6,72,128]{2,1,0:T(8,128)(2,1)S(1)} %slice.57), channel_id=1, source_target_pairs={{0,0},{1,1},{2,8},{3,9},{4,16},{5,17},{6,24},{7,25},{8,2},{9,3},{1... | collective-permute-start | bytes 331784 | tf_op jit(solution)/shard_map/ppermute | solution.py:311
  154.6 10.4 %collective-permute-start.2 = (bf16[6,20,128]{2,1,0:T(8,128)(2,1)S(1)}, bf16[6,20,128]{2,1,0:T(8,128)(2,1)S(1)}, u32[]{:S(2)}, u32[]{:S(2)}) collective-permute-start(bf16[6,20,128]{2,1,0:T(8,128)(2,1)S(1)} %slice.58), channel_id=1, source_target_pairs={{0,1},{1,2},{2,9},{3,10},{4,17},{5,18},{6,25},{7,26},{8,3},{9,4},{... | collective-permute-start | bytes 92168 | tf_op jit(solution)/shard_map/ppermute | solution.py:311

commit v5 on v4

--- a/solution.py
+++ b/solution.py
@@ -171,7 +171,7 @@
 
 def place_first(placing, tiles, terms):
     slots, tile_count = placing.shape
-    steps = 9
+    steps = 3
     width = (FIRST + 1) * SIDE // steps
     return pl.pallas_call(
         place_kernel,

time: 167 us -> 164 us (0.982)
  Pallas kernels: 57.2 us -> 54.5 us
    pallas_call x1, Pallas kernels: 7.66 us -> 4.93 us  [place_first(): pl.pallas_call(place_kernel, grid=(steps,), out_shape=jax.ShapeDtypeStruc...]
where the time goes in v5:
time: 164 us; the launch traced here: 163 us
  Pallas kernels  54.5 us (33%)
  waiting for transfers between devices  45.9 us (28%)
  starting transfers between devices  36.6 us (22%)
  local copies, waits for them, and re-layouts  10.3 us (6%)
  other arithmetic  9.51 us (6%)
  matrix products  6.03 us (4%)
    pallas_call x2, Pallas kernels, filter_tiles(): pl.pallas_call(functools.partial(filter_kernel, final, lines), grid=(step...  49.5 us
    all_to_all x2, waiting for transfers between devices, exchange(): lax.all_to_all(values, ('visit', 'core'), split_axis=0, concat_axis=0, ti...  32.7 us
    ppermute x5, starting transfers between devices, to_owner(): return lax.ppermute(values, every, pairs).astype(jnp.float32)  17 us
    all_to_all x2, starting transfers between devices, to_shares(): parts = lax.all_to_all(values, 'z', split_axis=0, concat_axis=0, tiled=True)  9.84 us
    all_to_all x2, starting transfers between devices, exchange(): lax.all_to_all(values, ('visit', 'core'), split_axis=0, concat_axis=0, ti...  9.72 us
    all_to_all x2, waiting for transfers between devices, to_shares(): parts = lax.all_to_all(values, 'z', split_axis=0, concat_axis=0, tiled=True)  6.94 us
    ppermute x5, waiting for transfers between devices, to_owner(): return lax.ppermute(values, every, pairs).astype(jnp.float32)  6.24 us
    pallas_call x1, Pallas kernels, place_first(): pl.pallas_call(place_kernel, grid=(steps,), out_shape=jax.ShapeDtypeStruc...  4.93 us
  transfers between devices with their start and end apart: 9, of which 3 were waited for; matrix products, arithmetic and copies ran while one was open for 9% of the time, Pallas kernels for 30%

profile of v5, /device:TPU:3, one launch (start us, length us, event | category | flops | bytes accessed | tf_op | source)
XLA Modules:
  0.0 163.0 jit_solution(164683321931562403)
XLA Ops:
  0.0 0.0 copy-start
  0.0 0.7 fusion.10
  0.8 0.1 reduce_window_sum.11
  0.9 0.8 select_reduce_fusion
  1.7 0.7 add_add_fusion
  2.4 0.6 fusion.8.placing_ref
  3.0 0.7 convert_bitcast_fusion
  3.7 0.1 copy.28
  3.8 0.7 fusion.11
  4.6 0.8 copy.27
  5.4 0.7 multiply_convert_fusion
  6.1 0.1 pad.30.clone
  6.2 0.7 maximum_maximum_fusion.terms_ref
  6.9 4.9 %shard_map.73 = bf16[192,10368]{1,0:T(8,128)(2,1)} custom-call(bf16[192,96]{1,0:T(8,128)(2,1)} %fusion.8.placing_ref, bf16[96,16384]{1,0:T(8,128)(2,1)} %tiles_ref.1, bf16[96,128]{1,0:T(8,128)(2,1)} %maximum_maximum_fusion.terms_ref), custom_call_target="tpu_custom_call" | custom-call | flops 382205952 | bytes 5971968 | tf_op jit(solution)/shard_map/pallas_call | solution.py:176
  11.8 4.6 %all-to-all-start = ((bf16[8,24,10368]{2,1,0:T(8,128)(2,1)}), bf16[8,24,10368]{2,1,0:T(8,128)(2,1)}, u32[]{:S(2)}, u32[]{:S(2)}) async-start(bf16[8,24,10368]{2,1,0:T(8,128)(2,1)} %bitcast.39), calls=%async_computation | async-start | bytes 7962624 | tf_op jit(solution)/shard_map/all_to_all | solution.py:262
  16.4 0.0 copy-done
  16.4 1.5 fusion
  17.9 0.0 copy-start.2
  17.9 1.9 %copy.43 = bf16[256,128,27]{1,0,2:T(8,128)(2,1)} copy(bf16[256,128,27]{1,2,0:T(8,128)(2,1)S(1)} %fusion) | data formatting | bytes 3538944 | tf_op jit(solution)/shard_map/qrj,bj->bqr/dot_general | solution.py:38
  19.8 0.0 copy-done.2
  19.9 1.0 fusion.6
  20.9 0.5 copy.32
  21.4 0.2 slice.56
  21.6 0.3 copy.36
  21.9 0.9 copy.37.row_ref
  22.8 1.2 copy.33
  24.0 1.5 copy.35.row_ref
  25.5 3.5 %convolution_convert_fusion = bf16[192,6144]{1,0:T(8,128)(2,1)} fusion(bf16[96,16384]{1,0:T(8,128)(2,1)} %tiles_ref.1, s32[96]{0:T(128)S(1)} %add_add_fusion), kind=kOutput, calls=%fused_computation | convolution fusion | flops 227690496 | bytes 3539328 | tf_op jit(solution)/shard_map/dot_general | solution.py:259
  29.0 32.7 %all-to-all-done = bf16[8,24,10368]{2,1,0:T(8,128)(2,1)} async-done(((bf16[8,24,10368]{2,1,0:T(8,128)(2,1)}), bf16[8,24,10368]{2,1,0:T(8,128)(2,1)}, u32[]{:S(2)}, u32[]{:S(2)}) %all-to-all-start) | async-done | bytes 3981344 | tf_op jit(solution)/shard_map/all_to_all | solution.py:262
  61.7 0.9 slice_bitcast_fusion.1
  62.6 0.8 slice_bitcast_fusion
  63.4 1.0 convert_reduce_fusion
  64.4 0.1 copy.30
  64.4 0.1 copy.29
  64.6 5.2 %all-to-all-start.2 = ((bf16[8,24,6144]{2,1,0:T(8,128)(2,1)}), bf16[8,24,6144]{2,1,0:T(8,128)(2,1)S(1)}, u32[]{:S(2)}, u32[]{:S(2)}) async-start(bf16[8,24,6144]{2,1,0:T(8,128)(2,1)} %bitcast.16), calls=%async_computation.2 | async-start | bytes 4718592 | tf_op jit(solution)/shard_map/all_to_all | solution.py:262
  69.7 0.9 multiply_reduce_fusion
  70.7 0.1 copy.39
  70.8 0.8 broadcast_multiply_fusion
  71.5 0.8 broadcast_in_dim.10.rest_0_
  72.3 29.8 %shard_map.74 = (bf16[24,80,128]{2,1,0:T(8,128)(2,1)}, f32[96,3200]{1,0:T(8,128)}) custom-call(bf16[648,192]{1,0:T(8,128)(2,1)} %bitcast.50, bf16[192,10368]{1,0:T(8,128)(2,1)} %bitcast.3.got_ref, bf16[27,256,128]{2,1,0:T(8,128)(2,1)} %bitcast.47, bf16[3,176,720]{2,1,0:T(8,128)(2,1)} %copy.35.row_ref, f32[24,16,128]{2,1,0:T(8,128)} %broadcast_in_dim.10.rest_0_), custom_call_target="tpu_custom_call" | custom-call | flops 16000000000 | bytes 8000000 | tf_op jit(solution)/shard_map/pallas_call | solution.py:227
  102.1 0.0 all-to-all-done.2
  102.1 0.0 copy-start.1
  102.2 5.3 %all-to-all-start.1 = ((bf16[24,80,128]{2,1,0:T(8,128)(2,1)}), bf16[24,80,128]{2,1,0:T(8,128)(2,1)S(1)}, u32[]{:S(2)}, u32[]{:S(2)}) async-start(bf16[24,80,128]{2,1,0:T(8,128)(2,1)} %get-tuple-element.10), calls=%async_computation.1 | async-start | bytes 983040 | tf_op jit(solution)/shard_map/all_to_all | solution.py:295
  107.5 0.0 copy-done.1
  107.5 19.7 %shard_map.75 = bf16[24,96,128]{2,1,0:T(8,128)(2,1)} custom-call(bf16[648,192]{1,0:T(8,128)(2,1)} %bitcast.51, bf16[192,6144]{1,0:T(8,128)(2,1)} %bitcast.43, bf16[27,256,128]{2,1,0:T(8,128)(2,1)} %bitcast.48, bf16[3,96,432]{2,1,0:T(8,128)(2,1)} %copy.37.row_ref, f32[96,3200]{1,0:T(8,128)} %get-tuple-element.12.rest_0_), custom_call_target="tpu_custom_call" | custom-call | flops 9600000000 | bytes 4800000 | tf_op jit(solution)/shard_map/pallas_call | solution.py:227
  127.2 0.0 all-to-all-done.1
  127.2 4.5 %all-to-all-start.3 = ((bf16[24,96,128]{2,1,0:T(8,128)(2,1)}), bf16[24,96,128]{2,1,0:T(8,128)(2,1)S(1)}, u32[]{:S(2)}, u32[]{:S(2)}) async-start(bf16[24,96,128]{2,1,0:T(8,128)(2,1)} %shard_map.75), calls=%async_computation.3 | async-start | bytes 1179648 | tf_op jit(solution)/shard_map/all_to_all | solution.py:295
  131.7 3.2 %collective-permute-start.4 = (f32[6,128]{1,0:T(8,128)S(1)}, f32[6,128]{1,0:T(8,128)S(1)}, u32[]{:S(2)}, u32[]{:S(2)}) collective-permute-start(f32[6,128]{1,0:T(8,128)S(1)} %convert_reduce_fusion.1), channel_id=1, source_target_pairs={{0,0},{1,1},{2,8},{3,9},{4,16},{5,17},{6,24},{7,25},{8,2},{9,3},{1... | collective-permute-start | bytes 9224 | tf_op jit(solution)/shard_map/ppermute | solution.py:311
  134.9 0.1 reduce_sum.56
  135.0 3.0 %collective-permute-start = (bf16[6,56,128]{2,1,0:T(8,128)(2,1)S(1)}, bf16[6,56,128]{2,1,0:T(8,128)(2,1)S(1)}, u32[]{:S(2)}, u32[]{:S(2)}) collective-permute-start(bf16[6,56,128]{2,1,0:T(8,128)(2,1)S(1)} %slice.55), channel_id=1, source_target_pairs={{0,0},{1,1},{2,8},{3,9},{4,16},{5,17},{6,24},{7,25},{8,2},{9,3},{1... | collective-permute-start | bytes 258056 | tf_op jit(solution)/shard_map/ppermute | solution.py:311
  138.0 4.8 %collective-permute-start.3 = (bf16[6,20,128]{2,1,0:T(8,128)(2,1)S(1)}, bf16[6,20,128]{2,1,0:T(8,128)(2,1)S(1)}, u32[]{:S(2)}, u32[]{:S(2)}) collective-permute-start(bf16[6,20,128]{2,1,0:T(8,128)(2,1)S(1)} %slice.59), channel_id=1, source_target_pairs={{1,0},{3,8},{5,16},{7,24},{8,1},{9,2},{10,9},{11,10},{12,17},{13,1... | collective-permute-start | bytes 92168 | tf_op jit(solution)/shard_map/ppermute | solution.py:311
  142.9 6.9 %all-to-all-done.3 = bf16[24,96,128]{2,1,0:T(8,128)(2,1)S(1)} async-done(((bf16[24,96,128]{2,1,0:T(8,128)(2,1)}), bf16[24,96,128]{2,1,0:T(8,128)(2,1)S(1)}, u32[]{:S(2)}, u32[]{:S(2)}) %all-to-all-start.3) | async-done | bytes 589856 | tf_op jit(solution)/shard_map/all_to_all | solution.py:295
  149.8 0.1 reduce_sum.57
  149.9 1.9 %collective-permute-start.1 = (bf16[6,72,128]{2,1,0:T(8,128)(2,1)S(1)}, bf16[6,72,128]{2,1,0:T(8,128)(2,1)S(1)}, u32[]{:S(2)}, u32[]{:S(2)}) collective-permute-start(bf16[6,72,128]{2,1,0:T(8,128)(2,1)S(1)} %slice.57), channel_id=1, source_target_pairs={{0,0},{1,1},{2,8},{3,9},{4,16},{5,17},{6,24},{7,25},{8,2},{9,3},{1... | collective-permute-start | bytes 331784 | tf_op jit(solution)/shard_map/ppermute | solution.py:311
  151.9 4.1 %collective-permute-start.2 = (bf16[6,20,128]{2,1,0:T(8,128)(2,1)S(1)}, bf16[6,20,128]{2,1,0:T(8,128)(2,1)S(1)}, u32[]{:S(2)}, u32[]{:S(2)}) collective-permute-start(bf16[6,20,128]{2,1,0:T(8,128)(2,1)S(1)} %slice.58), channel_id=1, source_target_pairs={{0,1},{1,2},{2,9},{3,10},{4,17},{5,18},{6,25},{7,26},{8,3},{9,4},{... | collective-permute-start | bytes 92168 | tf_op jit(solution)/shard_map/ppermute | solution.py:311
  156.0 0.0 collective-permute-done.4
  156.0 0.0 collective-permute-done.3
  156.0 0.0 collective-permute-done
  156.0 6.2 %collective-permute-done.2 = bf16[6,20,128]{2,1,0:T(8,128)(2,1)S(1)} collective-permute-done((bf16[6,20,128]{2,1,0:T(8,128)(2,1)S(1)}, bf16[6,20,128]{2,1,0:T(8,128)(2,1)S(1)}, u32[]{:S(2)}, u32[]{:S(2)}) %collective-permute-start.2) | collective-permute-done | bytes 30752 | tf_op jit(solution)/shard_map/ppermute | solution.py:311
  162.2 0.0 collective-permute-done.1
  162.3 0.8 divide_bitcast_fusion
  (12 shorter events, 0.1 us)
Async XLA Ops:
  0.0 16.4 %copy-start = (bf16[27,41]{1,0:T(8,128)(2,1)S(1)}, bf16[27,41]{1,0:T(8,128)(2,1)}, u32[]{:S(2)}) copy-start(bf16[27,41]{1,0:T(8,128)(2,1)} %param.13) | copy-start | bytes 6646
  11.8 49.9 %all-to-all-start = ((bf16[8,24,10368]{2,1,0:T(8,128)(2,1)}), bf16[8,24,10368]{2,1,0:T(8,128)(2,1)}, u32[]{:S(2)}, u32[]{:S(2)}) async-start(bf16[8,24,10368]{2,1,0:T(8,128)(2,1)} %bitcast.39), calls=%async_computation | async-start | bytes 7962624 | tf_op jit(solution)/shard_map/all_to_all | solution.py:262
  17.9 1.9 %copy-start.2 = (bf16[27,41]{1,0:T(8,128)(2,1)S(1)}, bf16[27,41]{1,0:T(8,128)(2,1)}, u32[]{:S(2)}) copy-start(bf16[27,41]{1,0:T(8,128)(2,1)} %param.12) | copy-start | bytes 6646
  64.6 37.6 %all-to-all-start.2 = ((bf16[8,24,6144]{2,1,0:T(8,128)(2,1)}), bf16[8,24,6144]{2,1,0:T(8,128)(2,1)S(1)}, u32[]{:S(2)}, u32[]{:S(2)}) async-start(bf16[8,24,6144]{2,1,0:T(8,128)(2,1)} %bitcast.16), calls=%async_computation.2 | async-start | bytes 4718592 | tf_op jit(solution)/shard_map/all_to_all | solution.py:262
  102.1 5.3 %copy-start.1 = (bf16[8,24,6144]{2,1,0:T(8,128)(2,1)}, bf16[8,24,6144]{2,1,0:T(8,128)(2,1)S(1)}, u32[]{:S(2)}) copy-start(bf16[8,24,6144]{2,1,0:T(8,128)(2,1)S(1)} %all-to-all-done.2) | copy-start | bytes 7077892
  102.2 25.0 %all-to-all-start.1 = ((bf16[24,80,128]{2,1,0:T(8,128)(2,1)}), bf16[24,80,128]{2,1,0:T(8,128)(2,1)S(1)}, u32[]{:S(2)}, u32[]{:S(2)}) async-start(bf16[24,80,128]{2,1,0:T(8,128)(2,1)} %get-tuple-element.10), calls=%async_computation.1 | async-start | bytes 983040 | tf_op jit(solution)/shard_map/all_to_all | solution.py:295
  127.2 22.6 %all-to-all-start.3 = ((bf16[24,96,128]{2,1,0:T(8,128)(2,1)}), bf16[24,96,128]{2,1,0:T(8,128)(2,1)S(1)}, u32[]{:S(2)}, u32[]{:S(2)}) async-start(bf16[24,96,128]{2,1,0:T(8,128)(2,1)} %shard_map.75), calls=%async_computation.3 | async-start | bytes 1179648 | tf_op jit(solution)/shard_map/all_to_all | solution.py:295
  131.7 24.3 %collective-permute-start.4 = (f32[6,128]{1,0:T(8,128)S(1)}, f32[6,128]{1,0:T(8,128)S(1)}, u32[]{:S(2)}, u32[]{:S(2)}) collective-permute-start(f32[6,128]{1,0:T(8,128)S(1)} %convert_reduce_fusion.1), channel_id=1, source_target_pairs={{0,0},{1,1},{2,8},{3,9},{4,16},{5,17},{6,24},{7,25},{8,2},{9,3},{1... | collective-permute-start | bytes 9224 | tf_op jit(solution)/shard_map/ppermute | solution.py:311
  135.0 21.0 %collective-permute-start = (bf16[6,56,128]{2,1,0:T(8,128)(2,1)S(1)}, bf16[6,56,128]{2,1,0:T(8,128)(2,1)S(1)}, u32[]{:S(2)}, u32[]{:S(2)}) collective-permute-start(bf16[6,56,128]{2,1,0:T(8,128)(2,1)S(1)} %slice.55), channel_id=1, source_target_pairs={{0,0},{1,1},{2,8},{3,9},{4,16},{5,17},{6,24},{7,25},{8,2},{9,3},{1... | collective-permute-start | bytes 258056 | tf_op jit(solution)/shard_map/ppermute | solution.py:311
  138.0 18.0 %collective-permute-start.3 = (bf16[6,20,128]{2,1,0:T(8,128)(2,1)S(1)}, bf16[6,20,128]{2,1,0:T(8,128)(2,1)S(1)}, u32[]{:S(2)}, u32[]{:S(2)}) collective-permute-start(bf16[6,20,128]{2,1,0:T(8,128)(2,1)S(1)} %slice.59), channel_id=1, source_target_pairs={{1,0},{3,8},{5,16},{7,24},{8,1},{9,2},{10,9},{11,10},{12,17},{13,1... | collective-permute-start | bytes 92168 | tf_op jit(solution)/shard_map/ppermute | solution.py:311
  149.9 12.3 %collective-permute-start.1 = (bf16[6,72,128]{2,1,0:T(8,128)(2,1)S(1)}, bf16[6,72,128]{2,1,0:T(8,128)(2,1)S(1)}, u32[]{:S(2)}, u32[]{:S(2)}) collective-permute-start(bf16[6,72,128]{2,1,0:T(8,128)(2,1)S(1)} %slice.57), channel_id=1, source_target_pairs={{0,0},{1,1},{2,8},{3,9},{4,16},{5,17},{6,24},{7,25},{8,2},{9,3},{1... | collective-permute-start | bytes 331784 | tf_op jit(solution)/shard_map/ppermute | solution.py:311
  151.9 10.4 %collective-permute-start.2 = (bf16[6,20,128]{2,1,0:T(8,128)(2,1)S(1)}, bf16[6,20,128]{2,1,0:T(8,128)(2,1)S(1)}, u32[]{:S(2)}, u32[]{:S(2)}) collective-permute-start(bf16[6,20,128]{2,1,0:T(8,128)(2,1)S(1)} %slice.58), channel_id=1, source_target_pairs={{0,1},{1,2},{2,9},{3,10},{4,17},{5,18},{6,25},{7,26},{8,3},{9,4},{... | collective-permute-start | bytes 92168 | tf_op jit(solution)/shard_map/ppermute | solution.py:311
